TPU v7x, 256 devices: a whole 4x4x8 slice. The times are simulated.
256 devices in a mesh: lon: 16 (over z, y_lo), lat: 16 (over y_hi, x, core).
Axes of the slice: x: 4, y: 4 (y_hi: 2, y_lo: 2; y = y_hi * 2 + y_lo), z: 8, core: 2. Of those that a mesh axis runs over, the one named last changes fastest.
Arguments:
- x_codes: bfloat16 [160, 128, 2048], P(None, 'lat', 'lon'), may hold values from -6 to 6
- x_scale: float32 [160, 128], P(None, 'lat'), may hold values from 0.3 to 3
- h_codes: bfloat16 [160, 128, 2048], P(None, 'lat', 'lon'), may hold values from -6 to 6
- h_scale: float32 [160, 128], P(None, 'lat'), may hold values from 0.3 to 3
- grad_out: bfloat16 [160, 128, 2048], P(None, 'lat', 'lon'), may hold values from -6 to 6
- land: int32 [128, 2048], P('lat', 'lon'), may hold values 0 or 1
- partner: int32 [2048], replicated, may hold values from 0 to 2047, as said below
- w_first: bfloat16 [3, 3, 160, 160], P(None, None, 'lat', 'lon'), may hold values from -0.15625 to 0.15625
- w_second: bfloat16 [3, 3, 160, 160], P(None, None, 'lat', 'lon'), may hold values from -0.15625 to 0.15625
Outputs:
- grad_in: float32 [160, 128, 2048], P(None, 'lat', 'lon')
- grad_first: float32 [3, 3, 160, 160], P(None, None, 'lat', 'lon')
- grad_second: float32 [3, 3, 160, 160], P(None, None, 'lat', 'lon')
Inputs may be any that keep to these rules, and one draw needn't show every extreme that they name: partner[i] = (2 p - 1 - i) mod 2048 for one pivot column p, so partner[partner[i]] = i.
All inputs are finite; a program needn't handle non-finite values. No bound on the sum of `land` on one device may be relied on, other than what follows from the above.
Results may differ from a plain program's by a relative error of at most 0.0041.
Values may be sent and summed in bfloat16 or wider, within the bound.
A program may use at most 64 MiB of HBM per device.

v0:
```python
import math

import jax
import jax.numpy as jnp
from jax import lax
from jax.sharding import PartitionSpec as P


def with_halo(value, sides, width, wrap):
    for axis, dim in sides:
        devices, length = (lax.axis_size(axis), value.shape[dim])
        up = [(i, (i + 1) % devices) for i in range(devices if wrap else devices - 1)]
        down = [(j, i) for i, j in up]
        last = lax.slice_in_dim(value, length - width, length, axis=dim)
        first = lax.slice_in_dim(value, 0, width, axis=dim)
        before = lax.ppermute(last, axis, up)
        after = lax.ppermute(first, axis, down)
        value = jnp.concatenate([before, value, after], axis=dim)
    return value


def gelu_parts(h):
    k = math.sqrt(2.0 / math.pi)
    tanh_part = jnp.tanh(k * (h + 0.044715 * h * h * h))
    value = 0.5 * h * (1.0 + tanh_part)
    slope = 0.5 * (1.0 + tanh_part) + 0.5 * h * (1.0 - tanh_part * tanh_part) * k * (
        1.0 + 3.0 * 0.044715 * h * h
    )
    return (value, slope)


def surround(field):
    wide = with_halo(field, (("lon", 2),), 1, True)
    return with_halo(wide, (("lat", 1),), 1, False)


def top_row(field):
    return lax.all_gather(field[:, -1, :], "lon", axis=1, tiled=True)


def is_top():
    return lax.axis_index("lat") == lax.axis_size("lat") - 1


def extend(field, partner):
    full = surround(field)
    row = top_row(field)
    width = field.shape[2]
    ncols = row.shape[1]
    begin = lax.axis_index("lon") * width
    index = (begin - 1 + jnp.arange(width + 2, dtype=jnp.int32)) % ncols
    north = jnp.take(row, jnp.take(partner, index), axis=1)
    last = jnp.where(is_top(), north, full[:, -1, :])
    return jnp.concatenate([full[:, :-1, :], last[:, None, :]], axis=1)


def weight_grad(grad, ext, factor):
    height, width = (grad.shape[1], grad.shape[2])
    rows = []
    for ka in range(3):
        cols = []
        for kb in range(3):
            cols.append(
                jnp.einsum(
                    "ohw,chw->oc",
                    grad,
                    ext[:, ka : ka + height, kb : kb + width],
                    preferred_element_type=jnp.float32,
                )
            )
        rows.append(jnp.stack(cols))
    return jnp.stack(rows) * factor


def reduce_weights(grad):
    part_sum = lax.psum_scatter(grad, "lat", scatter_dimension=2, tiled=True)
    return lax.psum_scatter(part_sum, "lon", scatter_dimension=3, tiled=True)


def input_grad(grad, weight, partner):
    height, width = (grad.shape[1], grad.shape[2])
    begin = lax.axis_index("lon") * width
    own_cols = begin + jnp.arange(width, dtype=jnp.int32)
    mirror = jnp.take(partner, own_cols)
    ext = surround(grad)
    result = jnp.zeros((weight.shape[3], height, width), jnp.float32)
    for ka in range(3):
        for kb in range(3):
            result = result + jnp.einsum(
                "oc,ohw->chw",
                weight[ka, kb],
                ext[:, 2 - ka : 2 - ka + height, 2 - kb : 2 - kb + width],
                preferred_element_type=jnp.float32,
            )
    row = top_row(grad)
    ncols = row.shape[1]
    folded = jnp.zeros((weight.shape[3], width), jnp.float32)
    for kb in range(3):
        picked = jnp.take(row, (mirror - kb + 1) % ncols, axis=1)
        folded = folded + jnp.einsum(
            "oc,ol->cl", weight[2, kb], picked, preferred_element_type=jnp.float32
        )
    folded = jnp.where(is_top(), folded, jnp.zeros_like(folded))
    return result.at[:, -1, :].add(folded)


def body(x_codes, x_scale, h_codes, h_scale, grad_out, land, partner, w_first, w_second):
    first_full, second_full = (
        lax.all_gather(w_first, "lat", axis=2, tiled=True),
        lax.all_gather(w_second, "lat", axis=2, tiled=True),
    )
    first_full, second_full = (
        lax.all_gather(first_full, "lon", axis=3, tiled=True),
        lax.all_gather(second_full, "lon", axis=3, tiled=True),
    )
    ocean = land.astype(jnp.float32)
    x = (x_codes.astype(jnp.float32) * x_scale[:, :, None]).astype(jnp.bfloat16)
    h = h_codes.astype(jnp.float32) * h_scale[:, :, None]
    value, slope = gelu_parts(h)
    act = (ocean * value).astype(jnp.bfloat16)
    grad_y = (ocean * grad_out.astype(jnp.float32)).astype(jnp.bfloat16)
    cells = x_codes.shape[1] * x_codes.shape[2] * lax.axis_size("lat") * lax.axis_size("lon")
    factor = 1.0 / math.sqrt(cells)
    grad_second = reduce_weights(weight_grad(grad_y, extend(act, partner), factor))
    grad_act = input_grad(grad_y, second_full, partner)
    grad_h = (grad_act * ocean * slope).astype(jnp.bfloat16)
    grad_first = reduce_weights(weight_grad(grad_h, extend(x, partner), factor))
    grad_in = grad_out.astype(jnp.float32) + input_grad(grad_h, first_full, partner)
    return (grad_in, grad_first, grad_second)


def solution(mesh):
    placed = (
        P(None, "lat", "lon"),
        P(None, "lat"),
        P(None, "lat", "lon"),
        P(None, "lat"),
        P(None, "lat", "lon"),
        P("lat", "lon"),
        P(),
        P(None, None, "lat", "lon"),
        P(None, None, "lat", "lon"),
    )
    return jax.shard_map(
        body,
        mesh=mesh,
        in_specs=placed,
        out_specs=(P(None, "lat", "lon"), P(None, None, "lat", "lon"), P(None, None, "lat", "lon")),
        check_vma=False,
    )
```

profile of v0, /device:TPU:6, one launch (start us, length us, event | category | flops | bytes accessed | tf_op | source)
XLA Modules:
  0.0 711.0 jit_solution(13825122716920749915)
XLA Ops:
  10.0 1.6 collective-permute-start
  11.6 5.3 collective-permute-start.1
  18.1 4.1 collective-permute-start.9
  22.2 20.1 %all_gather.24 = bf16[3,3,160,10]{3,1,0,2:T(4,128)(2,1)S(1)} all-gather(bf16[3,3,10,10]{3,1,0,2:T(4,128)(2,1)S(1)} %copy.49), channel_id=1, replica_groups=mesh['lon'=16,'lat'=16] {'lat'}, dimensions={2}, use_global_device_ids=true | all-gather | bytes 30600 | tf_op jit(solution)/shard_map/all_gather | solution.py:110
  42.7 38.4 %all_gather.25 = bf16[3,3,160,160]{2,1,0,3:T(4,128)(2,1)S(1)} all-gather(bf16[3,3,160,10]{2,1,0,3:T(4,128)(2,1)S(1)} %copy.50), channel_id=1, replica_groups=mesh['lon'=16,'lat'=16] {'lon'}, dimensions={3}, use_global_device_ids=true | all-gather | bytes 489600 | tf_op jit(solution)/shard_map/all_gather | solution.py:114
  81.1 2.1 fusion.151
  85.4 37.4 %all-gather = bf16[160,1,2048]{2,0,1:T(8,128)(2,1)} all-gather(bf16[160,1,128]{2,0,1:T(8,128)(2,1)S(1)} %slice.397), channel_id=2, replica_groups=mesh['lon'=16,'lat'=16] {'lon'}, dimensions={2}, use_global_device_ids=true | all-gather | bytes 696320 | tf_op jit(solution)/shard_map/all_gather | solution.py:38
  122.8 1.4 copy.60
  124.3 1.5 gather_fusion.1
  125.7 1.5 gather_fusion.2
  127.2 1.4 gather_fusion.7
  128.7 36.1 %all-gather.2 = bf16[160,1,2048]{2,0,1:T(8,128)(2,1)} all-gather(bf16[160,1,128]{2,0,1:T(8,128)(2,1)S(1)} %slice-done), channel_id=4, replica_groups=mesh['lon'=16,'lat'=16] {'lon'}, dimensions={2}, use_global_device_ids=true | all-gather | bytes 696320 | tf_op jit(solution)/shard_map/all_gather | solution.py:38
  164.8 22.4 %all_gather.27 = bf16[3,3,160,10]{3,1,0,2:T(4,128)(2,1)S(1)} all-gather(bf16[3,3,10,10]{3,1,0,2:T(4,128)(2,1)S(1)} %copy.64), channel_id=1, replica_groups=mesh['lon'=16,'lat'=16] {'lat'}, dimensions={2}, use_global_device_ids=true | all-gather | bytes 30600 | tf_op jit(solution)/shard_map/all_gather | solution.py:109
  187.6 39.1 %all_gather.28 = bf16[3,3,160,160]{2,1,0,3:T(4,128)(2,1)S(1)} all-gather(bf16[3,3,160,10]{2,1,0,3:T(4,128)(2,1)S(1)} %copy.65), channel_id=1, replica_groups=mesh['lon'=16,'lat'=16] {'lon'}, dimensions={3}, use_global_device_ids=true | all-gather | bytes 489600 | tf_op jit(solution)/shard_map/all_gather | solution.py:113
  226.7 2.1 fusion.150
  230.0 1.5 gather_fusion.3
  231.4 2.3 copy.79
  233.7 2.2 gather_fusion.8
  239.3 1.9 collective-permute-start.2
  241.2 2.4 collective-permute-start.3
  244.4 4.2 collective-permute-start.11
  248.6 5.7 collective-permute-start.10
  263.0 36.1 %all-gather.1 = bf16[160,1,2048]{2,0,1:T(8,128)(2,1)} all-gather(bf16[160,1,128]{2,0,1:T(8,128)(2,1)S(1)} %slice.415), channel_id=3, replica_groups=mesh['lon'=16,'lat'=16] {'lon'}, dimensions={2}, use_global_device_ids=true | all-gather | bytes 696320 | tf_op jit(solution)/shard_map/all_gather | solution.py:38
  299.0 1.4 copy.75
  300.4 1.5 gather_fusion.4
  301.9 1.5 gather_fusion.5
  304.3 1.5 gather_fusion.6
  305.8 1.6 collective-permute-start.12
  307.4 2.6 collective-permute-start.13
  309.9 44.7 %all-gather.3 = bf16[160,1,2048]{2,0,1:T(8,128)(2,1)} all-gather(bf16[160,1,128]{2,0,1:T(8,128)(2,1)S(1)} %slice.430), channel_id=5, replica_groups=mesh['lon'=16,'lat'=16] {'lon'}, dimensions={2}, use_global_device_ids=true | all-gather | bytes 696320 | tf_op jit(solution)/shard_map/all_gather | solution.py:38
  354.7 2.2 copy.83
  356.9 2.2 gather_fusion.9
  364.0 1.8 collective-permute-start.4
  366.0 1.9 collective-permute-start.15
  367.9 1.2 collective-permute-done.5
  369.2 2.0 collective-permute-start.14
  371.2 2.0 collective-permute-done.4
  374.0 1.9 collective-permute-start.6
  376.8 1.3 fusion.51
  378.1 2.6 collective-permute-start.7
  384.2 1.5 maximum_maximum_fusion.2
  388.1 2.3 copy.85
  390.4 2.3 copy.81
  392.7 1.5 pad_maximum_fusion.1
  398.9 147.5 %all-reduce.9.cloned.1.call-done = (f32[3,3,160,160]{3,1,0,2:T(4,128)}, f32[3,3,160,160]{3,1,0,2:T(4,128)}) async-done(((f32[3,3,160,160]{3,1,0,2:T(4,128)}, f32[3,3,160,160]{3,1,0,2:T(4,128)}), (f32[3,3,160,160]{3,1,0,2:T(4,128)}, f32[3,3,160,160]{3,1,0,2:T(4,128)})) %all-reduce.9.cloned.1.call-update) | async-done | bytes 1843216
  547.4 1.3 copy.82
  549.6 1.3 copy.86
  552.3 148.7 %all-reduce.11.cloned.1.call-done = (f32[3,3,10,160]{2,1,0,3:T(4,128)}, f32[3,3,10,160]{2,1,0,3:T(4,128)}) async-done(((f32[3,3,10,160]{2,1,0,3:T(4,128)}, f32[3,3,10,160]{2,1,0,3:T(4,128)}), (f32[3,3,10,160]{2,1,0,3:T(4,128)}, f32[3,3,10,160]{2,1,0,3:T(4,128)})) %all-reduce.11.cloned.1.call-update) | async-done | bytes 115216
  (206 shorter events, 43.9 us)
Async XLA Ops:
  7.2 77.1 %copy-start = (s32[2048]{0:T(1024)S(1)}, s32[2048]{0:T(1024)}, u32[]{:S(2)}) copy-start(s32[2048]{0:T(1024)} %param.27) | copy-start | bytes 24580
  7.2 9.7 %copy-start.28 = (bf16[160,8,128]{2,1,0:T(8,128)(2,1)S(1)}, bf16[160,8,128]{2,1,0:T(8,128)(2,1)}, u32[]{:S(2)}) copy-start(bf16[160,8,128]{2,1,0:T(8,128)(2,1)} %param.21) | copy-start | bytes 983044
  7.2 9.7 %copy-start.42 = (f32[160,8]{0,1:T(8,128)S(1)}, f32[160,8]{0,1:T(8,128)}, u32[]{:S(2)}) copy-start(f32[160,8]{0,1:T(8,128)} %param.22) | copy-start | bytes 15364
  7.2 539.2 %all-reduce.9.cloned.1.call-start = ((), (), s32[]{:S(2)}) async-start(), calls=%async_computation | async-start | bytes 7864320
  9.0 13.2 %copy-start.39 = (bf16[3,3,10,10]{3,1,2,0:T(4,128)(2,1)S(1)}, bf16[3,3,10,10]{3,1,2,0:T(4,128)(2,1)}, u32[]{:S(2)}) copy-start(bf16[3,3,10,10]{3,1,2,0:T(4,128)(2,1)} %param.29) | copy-start | bytes 5404
  10.0 229.1 %collective-permute-start = (bf16[160,8,1]{2,0,1:T(8,128)(2,1)}, bf16[160,8,1]{2,0,1:T(8,128)(2,1)S(1)}, u32[]{:S(2)}, u32[]{:S(2)}) collective-permute-start(bf16[160,8,1]{2,0,1:T(8,128)(2,1)} %get-tuple-element.95), channel_id=1, source_target_pairs={{0,16},{16,32},{32,48},{48,64},{64,80},{80,96},{96,112},{112,128},... | collective-permute-start | bytes 7688 | tf_op jit(solution)/shard_map/ppermute | solution.py:16
  11.6 227.5 %collective-permute-start.1 = (bf16[160,8,1]{2,0,1:T(8,128)(2,1)}, bf16[160,8,1]{2,0,1:T(8,128)(2,1)S(1)}, u32[]{:S(2)}, u32[]{:S(2)}) collective-permute-start(bf16[160,8,1]{2,0,1:T(8,128)(2,1)} %get-tuple-element.96), channel_id=1, source_target_pairs={{16,0},{32,16},{48,32},{64,48},{80,64},{96,80},{112,96},{128,112},... | collective-permute-start | bytes 7688 | tf_op jit(solution)/shard_map/ppermute | solution.py:17
  17.1 64.0 %copy-start.1 = (bf16[160,8,128]{2,0,1:T(8,128)(2,1)}, bf16[160,8,128]{2,0,1:T(8,128)(2,1)S(1)}, u32[]{:S(2)}) copy-start(bf16[160,8,128]{2,0,1:T(8,128)(2,1)S(1)} %multiply_convert_fusion.1) | copy-start | bytes 983044
  18.1 225.5 %collective-permute-start.8 = (bf16[160,8,1]{2,0,1:T(8,128)(2,1)}, bf16[160,8,1]{2,0,1:T(8,128)(2,1)S(1)}, u32[]{:S(2)}, u32[]{:S(2)}) collective-permute-start(bf16[160,8,1]{2,0,1:T(8,128)(2,1)} %get-tuple-element.91), channel_id=1, source_target_pairs={{0,16},{16,32},{32,48},{48,64},{64,80},{80,96},{96,112},{112,128},... | collective-permute-start | bytes 7688 | tf_op jit(solution)/shard_map/ppermute | solution.py:16
  18.1 225.5 %collective-permute-start.9 = (bf16[160,8,1]{2,0,1:T(8,128)(2,1)}, bf16[160,8,1]{2,0,1:T(8,128)(2,1)S(1)}, u32[]{:S(2)}, u32[]{:S(2)}) collective-permute-start(bf16[160,8,1]{2,0,1:T(8,128)(2,1)} %get-tuple-element.92), channel_id=1, source_target_pairs={{16,0},{32,16},{48,32},{64,48},{80,64},{96,80},{112,96},{128,112},... | collective-permute-start | bytes 7688 | tf_op jit(solution)/shard_map/ppermute | solution.py:17
  122.8 5.9 slice-start
  124.2 40.5 %copy-start.40 = (bf16[3,3,10,10]{3,1,2,0:T(4,128)(2,1)S(1)}, bf16[3,3,10,10]{3,1,2,0:T(4,128)(2,1)}, u32[]{:S(2)}) copy-start(bf16[3,3,10,10]{3,1,2,0:T(4,128)(2,1)} %param.28) | copy-start | bytes 5404
  226.7 2.2 copy-start.35
  226.7 2.4 copy-start.13
  226.7 2.4 copy-start.34
  230.0 6.6 copy-start.44
  230.0 7.2 %copy-start.43 = (u32[256]{0:T(256)S(1)}, u32[256]{0:T(256)}, u32[]{:S(2)}) copy-start(u32[256]{0:T(256)} %constant.182) | copy-start | bytes 3076
  231.4 12.2 %copy-start.2 = (bf16[160,8,128]{2,0,1:T(8,128)(2,1)S(1)}, bf16[160,8,128]{2,0,1:T(8,128)(2,1)}, u32[]{:S(2)}) copy-start(bf16[160,8,128]{2,0,1:T(8,128)(2,1)} %copy-done.1) | copy-start | bytes 983044
  233.7 20.6 %copy-start.22 = (bf16[1,1,160,160]{2,1,0,3:T(2,128)(2,1)S(1)}, bf16[1,1,160,160]{2,1,0,3:T(2,128)(2,1)}, u32[]{:S(2)}) copy-start(bf16[1,1,160,160]{2,1,0,3:T(2,128)(2,1)} %get-tuple-element.78) | copy-start | bytes 153604
  239.3 15.5 %collective-permute-start.2 = (bf16[160,1,130]{2,0,1:T(8,128)(2,1)S(1)}, bf16[160,1,130]{2,0,1:T(8,128)(2,1)S(1)}, u32[]{:S(2)}, u32[]{:S(2)}) collective-permute-start(bf16[160,1,130]{2,0,1:T(8,128)(2,1)S(1)} %get-tuple-element.85), channel_id=1, source_target_pairs={{1,0},{2,1},{3,2},{4,3},{5,4},{6,5},{7,6},{8,7},{9,8},{10,9},{11,1... | collective-permute-start | bytes 124808 | tf_op jit(solution)/shard_map/ppermute | solution.py:17
  241.2 13.6 %collective-permute-start.3 = (bf16[160,1,130]{2,0,1:T(8,128)(2,1)S(1)}, bf16[160,1,130]{2,0,1:T(8,128)(2,1)S(1)}, u32[]{:S(2)}, u32[]{:S(2)}) collective-permute-start(bf16[160,1,130]{2,0,1:T(8,128)(2,1)S(1)} %get-tuple-element.86), channel_id=1, source_target_pairs={{0,1},{1,2},{2,3},{3,4},{4,5},{5,6},{6,7},{7,8},{8,9},{9,10},{10,1... | collective-permute-start | bytes 124808 | tf_op jit(solution)/shard_map/ppermute | solution.py:16
  244.4 133.6 %collective-permute-start.11 = (bf16[160,1,130]{2,0,1:T(8,128)(2,1)}, bf16[160,1,130]{2,0,1:T(8,128)(2,1)}, u32[]{:S(2)}, u32[]{:S(2)}) collective-permute-start(bf16[160,1,130]{2,0,1:T(8,128)(2,1)} %get-tuple-element.60), channel_id=1, source_target_pairs={{1,0},{2,1},{3,2},{4,3},{5,4},{6,5},{7,6},{8,7},{9,8},{10,9},{11,1... | collective-permute-start | bytes 124808 | tf_op jit(solution)/shard_map/ppermute | solution.py:17
  248.6 135.6 %collective-permute-start.10 = (bf16[160,1,130]{2,0,1:T(8,128)(2,1)}, bf16[160,1,130]{2,0,1:T(8,128)(2,1)}, u32[]{:S(2)}, u32[]{:S(2)}) collective-permute-start(bf16[160,1,130]{2,0,1:T(8,128)(2,1)} %get-tuple-element.59), channel_id=1, source_target_pairs={{0,1},{1,2},{2,3},{3,4},{4,5},{5,6},{6,7},{7,8},{8,9},{9,10},{10,1... | collective-permute-start | bytes 124808 | tf_op jit(solution)/shard_map/ppermute | solution.py:16
  255.4 1.2 copy-start.19
  305.8 58.1 %collective-permute-start.12 = (bf16[160,8,1]{2,0,1:T(8,128)(2,1)}, bf16[160,8,1]{2,0,1:T(8,128)(2,1)S(1)}, u32[]{:S(2)}, u32[]{:S(2)}) collective-permute-start(bf16[160,8,1]{2,0,1:T(8,128)(2,1)} %get-tuple-element.89), channel_id=1, source_target_pairs={{0,16},{16,32},{32,48},{48,64},{64,80},{80,96},{96,112},{112,128},... | collective-permute-start | bytes 7688 | tf_op jit(solution)/shard_map/ppermute | solution.py:16
  307.4 52.6 %copy-start.18 = (bf16[1,1,160,160]{2,1,0,3:T(2,128)(2,1)S(1)}, bf16[1,1,160,160]{2,1,0,3:T(2,128)(2,1)}, u32[]{:S(2)}) copy-start(bf16[1,1,160,160]{2,1,0,3:T(2,128)(2,1)} %get-tuple-element.64) | copy-start | bytes 153604
  307.4 58.5 %collective-permute-start.13 = (bf16[160,8,1]{2,0,1:T(8,128)(2,1)}, bf16[160,8,1]{2,0,1:T(8,128)(2,1)S(1)}, u32[]{:S(2)}, u32[]{:S(2)}) collective-permute-start(bf16[160,8,1]{2,0,1:T(8,128)(2,1)} %get-tuple-element.90), channel_id=1, source_target_pairs={{16,0},{32,16},{48,32},{64,48},{80,64},{96,80},{112,96},{128,112},... | collective-permute-start | bytes 7688 | tf_op jit(solution)/shard_map/ppermute | solution.py:17
  356.9 5.3 copy-start.10
  356.9 5.3 copy-start.36
  359.8 9.4 %collective-permute-start.5 = (bf16[160,8,1]{2,0,1:T(8,128)(2,1)}, bf16[160,8,1]{2,0,1:T(8,128)(2,1)S(1)}, u32[]{:S(2)}, u32[]{:S(2)}) collective-permute-start(bf16[160,8,1]{2,0,1:T(8,128)(2,1)} %get-tuple-element.94), channel_id=1, source_target_pairs={{16,0},{32,16},{48,32},{64,48},{80,64},{96,80},{112,96},{128,112},... | collective-permute-start | bytes 7688 | tf_op jit(solution)/shard_map/ppermute | solution.py:17
  361.0 2.8 copy-start.15
  364.0 9.2 %collective-permute-start.4 = (bf16[160,8,1]{2,0,1:T(8,128)(2,1)S(1)}, bf16[160,8,1]{2,0,1:T(8,128)(2,1)S(1)}, u32[]{:S(2)}, u32[]{:S(2)}) collective-permute-start(bf16[160,8,1]{2,0,1:T(8,128)(2,1)S(1)} %copy-done.27), channel_id=1, source_target_pairs={{0,16},{16,32},{32,48},{48,64},{64,80},{80,96},{96,112},{112,128},... | collective-permute-start | bytes 7688 | tf_op jit(solution)/shard_map/ppermute | solution.py:16
  366.0 14.7 %collective-permute-start.15 = (bf16[160,1,130]{2,0,1:T(8,128)(2,1)S(1)}, bf16[160,1,130]{2,0,1:T(8,128)(2,1)S(1)}, u32[]{:S(2)}, u32[]{:S(2)}) collective-permute-start(bf16[160,1,130]{2,0,1:T(8,128)(2,1)S(1)} %get-tuple-element.56), channel_id=1, source_target_pairs={{1,0},{2,1},{3,2},{4,3},{5,4},{6,5},{7,6},{8,7},{9,8},{10,9},{11,1... | collective-permute-start | bytes 124808 | tf_op jit(solution)/shard_map/ppermute | solution.py:17
  369.2 7.6 %copy-start.21 = (bf16[1,1,160,160]{2,1,0,3:T(2,128)(2,1)S(1)}, bf16[1,1,160,160]{2,1,0,3:T(2,128)(2,1)}, u32[]{:S(2)}) copy-start(bf16[1,1,160,160]{2,1,0,3:T(2,128)(2,1)} %get-tuple-element.65) | copy-start | bytes 153604
  369.2 12.5 %collective-permute-start.14 = (bf16[160,1,130]{2,0,1:T(8,128)(2,1)S(1)}, bf16[160,1,130]{2,0,1:T(8,128)(2,1)S(1)}, u32[]{:S(2)}, u32[]{:S(2)}) collective-permute-start(bf16[160,1,130]{2,0,1:T(8,128)(2,1)S(1)} %get-tuple-element.55), channel_id=1, source_target_pairs={{0,1},{1,2},{2,3},{3,4},{4,5},{5,6},{6,7},{7,8},{8,9},{9,10},{10,1... | collective-permute-start | bytes 124808 | tf_op jit(solution)/shard_map/ppermute | solution.py:16
  373.2 3.5 copy-start.3
  374.0 18.7 %collective-permute-start.6 = (bf16[160,1,130]{2,0,1:T(8,128)(2,1)}, bf16[160,1,130]{2,0,1:T(8,128)(2,1)}, u32[]{:S(2)}, u32[]{:S(2)}) collective-permute-start(bf16[160,1,130]{2,0,1:T(8,128)(2,1)} %get-tuple-element.72), channel_id=1, source_target_pairs={{1,0},{2,1},{3,2},{4,3},{5,4},{6,5},{7,6},{8,7},{9,8},{10,9},{11,1... | collective-permute-start | bytes 124808 | tf_op jit(solution)/shard_map/ppermute | solution.py:17
  376.4 1.7 copy-start.14
  376.7 4.0 copy-start.32
  376.7 4.0 copy-start.33
  378.1 14.6 %collective-permute-start.7 = (bf16[160,1,130]{2,0,1:T(8,128)(2,1)}, bf16[160,1,130]{2,0,1:T(8,128)(2,1)S(1)}, u32[]{:S(2)}, u32[]{:S(2)}) collective-permute-start(bf16[160,1,130]{2,0,1:T(8,128)(2,1)} %get-tuple-element.73), channel_id=1, source_target_pairs={{0,1},{1,2},{2,3},{3,4},{4,5},{5,6},{6,7},{7,8},{8,9},{9,10},{10,1... | collective-permute-start | bytes 124808 | tf_op jit(solution)/shard_map/ppermute | solution.py:16
  390.4 2.3 copy-start.4
  392.7 1.6 copy-start.11
  394.6 1.5 copy-start.9
  394.6 306.3 %all-reduce.11.cloned.1.call-start = ((), (), s32[]{:S(2)}) async-start(), calls=%async_computation.1 | async-start | bytes 3932160
  395.5 1.3 copy-start.6
  395.5 1.3 copy-start.24
  549.6 1.4 copy-start.8
  (16 other events, 16.2 us)
Sparse Core Ops, SparseCore 0:
  394.7 151.6 all-reduce.8
  551.1 149.7 all-reduce.10
where the time goes:
time: 712 us; the launch traced here: 711 us
  waiting for transfers between devices  299 us (42%)
  blocking collectives  274 us (38%)
  local copies, waits for them, and re-layouts  51.9 us (7%)
  starting transfers between devices  39.9 us (6%)
  matrix products  18.9 us (3%)
  between operations  16.3 us (2%)
  other arithmetic  10.3 us (1%)
    unnamed x4, waiting for transfers between devices  296 us
    all_gather x4, blocking collectives, top_row(): return lax.all_gather(field[:, -1, :], 'lon', axis=1, tiled=True)  154 us
    all_gather x1, blocking collectives, body(): lax.all_gather(first_full, 'lon', axis=3, tiled=True)  39.1 us
    all_gather x1, blocking collectives, body(): lax.all_gather(second_full, 'lon', axis=3, tiled=True)  38.4 us
    all_gather x1, blocking collectives, body(): lax.all_gather(w_first, 'lat', axis=2, tiled=True)  22.4 us
    ppermute x8, starting transfers between devices, with_halo(): after = lax.ppermute(first, axis, down)  22.1 us
    all_gather x1, blocking collectives, body(): lax.all_gather(w_second, 'lat', axis=2, tiled=True)  20.1 us
    ppermute x8, starting transfers between devices, with_halo(): before = lax.ppermute(last, axis, up)  17.8 us
  transfers between devices with their start and end apart: 18, of which 4 were waited for; matrix products, arithmetic and copies ran while one was open for 9% of the time, Pallas kernels for 0%

commit v1 on v0

v1 whole, which is shorter than its diff:
```python
import functools
import math

import jax
import jax.numpy as jnp
from jax import lax
from jax.experimental import pallas as pl
from jax.experimental.pallas import tpu as pltpu
from jax.sharding import PartitionSpec as P

MESH = pl.DeviceIdType.MESH
F32, BF16 = jnp.float32, jnp.bfloat16
PAD = 16
LANES = 128
SUM_TYPE = jnp.float32


def up(value, unit):
    return -(-value // unit) * unit


def gelu_parts(h):
    k = math.sqrt(2.0 / math.pi)
    tanh_part = jnp.tanh(k * (h + 0.044715 * h * h * h))
    value = 0.5 * h * (1.0 + tanh_part)
    slope = 0.5 * (1.0 + tanh_part) + 0.5 * h * (1.0 - tanh_part * tanh_part) * k * (
        1.0 + 3.0 * 0.044715 * h * h
    )
    return (value, slope)


def dot(a, b):
    return lax.dot_general(a, b, (((1,), (0,)), ((), ())), preferred_element_type=F32)


def dot_nt(a, b):
    return lax.dot_general(a, b, (((1,), (1,)), ((), ())), preferred_element_type=F32)


def put(tiles, lane, source, source_lane, count, target_lane):
    shift = (target_lane - source_lane) % LANES
    moved = pltpu.roll(source, shift, 1) if shift else source
    tile, off = divmod(target_lane, LANES)
    keep = (lane >= off) & (lane < off + count)
    tiles[tile] = jnp.where(keep, moved, tiles[tile])
    over = off + count - LANES
    if over > 0:
        tiles[tile + 1] = jnp.where(lane < over, moved, tiles[tile + 1])


def put_wide(tiles, lane, sources, source_lane, count, target_lane):
    while count > 0:
        tile, off = divmod(source_lane, LANES)
        part = min(count, LANES - off)
        put(tiles, lane, sources[tile], off, part, target_lane)
        source_lane, target_lane, count = source_lane + part, target_lane + part, count - part


def kernel(
    cfg,
    x_ref, xs_ref, h_ref, hs_ref, g_ref, land_ref, partner_ref, w_ref,
    out_ref, first_ref, second_ref,
    cells, slope, wtile, wrow, wfull, wt, fy, fh, sa, sx, gx, ge, edge, edge_in,
    toprow, select, mcat, padder, qs, qe, tap, tap_in, part, part_in, small, small_in,
    st1_s, st1_r, st2_s, st2_r, fw_s, fw_r, ha_s, ha_r, mi_s, mi_r,
    r0_s, r0_r, r1_s, r1_r, r2_s, r2_r,
):
    C, H, NJ, NI = cfg["C"], cfg["H"], cfg["NJ"], cfg["NI"]
    W = LANES
    CJ, CI, NM = C // NJ, C // NI, NJ // 2
    LA = up(3 * C, LANES)
    ROWS = NJ * PAD
    N = H * W
    j, i = lax.axis_index("lat"), lax.axis_index("lon")
    k, m = lax.rem(j, 2), lax.div(j, 2)
    top = j == NJ - 1
    bottom = j == 0

    def rcopy(src, dst, ss, rs, dj, di):
        return pltpu.make_async_remote_copy(
            src_ref=src, dst_ref=dst, send_sem=ss, recv_sem=rs,
            device_id={"lat": dj, "lon": di}, device_id_type=MESH,
        )

    def each(lo, hi, fn):
        lax.fori_loop(lo, hi, lambda d, c: (fn(d), c)[1], 0)

    def lon(d):
        return lax.rem(i + d + NI, NI)

    def lat(d):
        return lax.rem(j + d + NJ, NJ)

    def mate(d):
        return lax.rem(m + d + NM, NM)

    barrier = pltpu.get_barrier_semaphore()

    def greet(dj, di):
        pl.semaphore_signal(barrier, inc=1, device_id={"lat": dj, "lon": di}, device_id_type=MESH)

    each(1, NI, lambda d: greet(j, lon(d)))
    each(1, NJ, lambda d: greet(lat(d), i))
    for dj in (1, -1):
        for di in (1, -1):
            greet(lat(dj), lon(di))

    def blocks(ref):
        cells[...] = ref[...].astype(F32).reshape(C * H, W)
        return [cells[pl.ds(r, C, stride=H), :] for r in range(H)]

    def ocean(r):
        return land_ref[r:r + 1, :].astype(F32)

    def slot(r):
        return pl.ds((r + 1) * W, W)

    lane = lax.broadcasted_iota(jnp.int32, (C, W), 1)

    def add_edges(packed, r, blk, base):
        west, east = base + r, base + H + r
        packed = jnp.where(lane == west, pltpu.roll(blk, west, 1) if west else blk, packed)
        return jnp.where(lane == east, pltpu.roll(blk, east + 1, 1), packed)

    pl.semaphore_wait(barrier, NI - 1 + NJ - 1 + 4)

    def tile_copy(d, other):
        return rcopy(w_ref, wtile.at[i if other is None else other], st1_s.at[d], st1_r.at[d], j, lon(d))

    each(1, NI, lambda d: tile_copy(d, None).start())
    wtile[i] = w_ref[...]

    packed = jnp.zeros((C, W), F32)
    for r, blk in enumerate(blocks(g_ref)):
        value = blk * ocean(r)
        fy[:, slot(r)] = value.astype(BF16)
        packed = add_edges(packed, r, value, 0)

    def top_copy(f, src, d, other):
        at = pl.ds(pl.multiple_of((i if other is None else other) * W, W), W)
        return rcopy(src, toprow.at[f, :, at], mi_s.at[f, d], mi_r.at[f, d], j, lon(d))

    def send_top(f, src):
        @pl.when(top)
        def _():
            each(1, NI, lambda d: top_copy(f, src, d, None).start())
            toprow[f, :, pl.ds(pl.multiple_of(i * W, W), W)] = src[...]

    center = pl.ds(C, C)
    send_top(0, fy.at[:, slot(H - 1)])

    for r, blk in enumerate(blocks(h_ref)):
        h = blk * hs_ref[:, r:r + 1]
        value, deriv = gelu_parts(h)
        act = (ocean(r) * value).astype(BF16)
        sa[center, slot(r)] = act
        slope[:, r * W:(r + 1) * W] = deriv
        packed = add_edges(packed, r, act.astype(F32), 2 * H)
    for r, blk in enumerate(blocks(x_ref)):
        x = (blk * xs_ref[:, r:r + 1]).astype(BF16)
        sx[center, slot(r)] = x
        packed = add_edges(packed, r, x.astype(F32), 4 * H)
    edge[0] = packed.astype(BF16)

    around = ((0, 1), (0, -1), (1, 1), (1, -1), (-1, 1), (-1, -1))

    def halo_copies(phase, fields):
        out = []
        for f, field in enumerate(fields):
            s = 2 * f
            out.append(rcopy(field.at[:, slot(H - 1)], field.at[:, slot(-1)],
                             ha_s.at[phase, s], ha_r.at[phase, s], lat(1), i))
            out.append(rcopy(field.at[:, slot(0)], field.at[:, slot(H)],
                             ha_s.at[phase, s + 1], ha_r.at[phase, s + 1], lat(-1), i))
        for n, (dj, di) in enumerate(around):
            out.append(rcopy(edge.at[phase], edge_in.at[phase, n],
                             ha_s.at[phase, 6 + n], ha_r.at[phase, 6 + n], lat(dj), lon(di)))
        return out

    early = halo_copies(0, (fy, sa.at[center], sx.at[center]))
    for copy in early:
        copy.start()
    send_top(1, sx.at[center, slot(H - 1)])

    row = lax.broadcasted_iota(jnp.int32, (ROWS, C), 0)
    col = lax.broadcasted_iota(jnp.int32, (ROWS, C), 1)
    half, rest = lax.div(row, NM * PAD), lax.rem(row, NM * PAD)
    own = lax.rem(rest, PAD)
    channel = (2 * lax.div(rest, PAD) + half) * CJ + own
    padder[...] = jnp.where((own < CJ) & (channel == col), 1.0, 0.0).astype(BF16)

    @pl.when(top)
    def _():
        ncols = NI * W
        mirror = partner_ref[pl.ds(i, 1), :]

        def fill(s, c):
            u = lax.broadcasted_iota(jnp.int32, (W, W), 0) + s * W
            for b in range(3):
                want = mirror + (1 - b)
                want = jnp.where(want < 0, want + ncols, want)
                want = jnp.where(want >= ncols, want - ncols, want)
                hot = jnp.where(u == want, 1.0, 0.0).astype(BF16)
                select[pl.ds(pl.multiple_of(s * W, W), W), b * W:(b + 1) * W] = hot
            return c

        lax.fori_loop(0, NI, fill, 0)

    each(1, NI, lambda d: tile_copy(d, lon(-d)).wait_recv())
    wlane = lax.broadcasted_iota(jnp.int32, (2 * PAD, W), 1)
    for a in range(3):
        tiles = [jnp.zeros((2 * PAD, W), F32) for _ in range(LA // W)]
        for s in range(NI):
            piece = wtile[s].astype(F32)
            for b in range(3):
                put(tiles, wlane, piece, (3 * a + b) * CI, CI, b * C + s * CI)
        for t, value in enumerate(tiles):
            at = pl.ds(a * LA + t * W, W)
            wrow[0, :, at] = value[:PAD].astype(BF16)
            wrow[1, :, at] = value[PAD:].astype(BF16)

    def slab_copy(w, d, other):
        return rcopy(wrow.at[w], wfull.at[w, k, m if other is None else other],
                     st2_s.at[w, d], st2_r.at[w, d], 2 * mate(d) + k, i)

    def forward_copy(w, d, mine):
        n = mate(-d)
        return rcopy(wfull.at[w, k, n], wfull.at[w, k if mine else 1 - k, n],
                     fw_s.at[w, d], fw_r.at[w, d], j + 1 - 2 * k, i)

    def own_forward(w, mine):
        return rcopy(wrow.at[w], wfull.at[w, k if mine else 1 - k, m], fw_s.at[w, 0], fw_r.at[w, 0],
                     j + 1 - 2 * k, i)

    for w in (1, 0):
        own_forward(w, True).start()
        each(1, NM, lambda d: slab_copy(w, d, None).start())
        wfull[w, k, m] = wrow[w]

    def pass_on(w):
        def step(d):
            slab_copy(w, d, mate(-d)).wait_recv()
            forward_copy(w, d, True).start()

        each(1, NM, step)

    def have_weights(w):
        own_forward(w, False).wait_recv()
        each(1, NM, lambda d: forward_copy(w, d, False).wait_recv())

    def columns(phase, base):
        got = [edge_in[phase, n].astype(F32) for n in range(6)]
        result = []
        for side, (mid, south, north) in ((0, (0, 2, 4)), (1, (1, 3, 5))):
            start = base + (H if side == 0 else 0)
            value = jnp.where((lane >= 1) & (lane <= H), pltpu.roll(got[mid], (1 - start) % W, 1), 0.0)
            lower = pltpu.roll(got[south], (0 - (start + H - 1)) % W, 1)
            upper = pltpu.roll(got[north], (H + 1 - start) % W, 1)
            value = jnp.where((lane == 0) & jnp.logical_not(bottom), lower, value)
            value = jnp.where((lane == H + 1) & jnp.logical_not(top), upper, value)
            result.append(value)
        return result

    def clear_ends(field):
        @pl.when(bottom)
        def _():
            field[:, slot(-1)] = jnp.zeros((C, W), BF16)

        @pl.when(top)
        def _():
            field[:, slot(H)] = jnp.zeros((C, W), BF16)

    def shifted(field, west, east):
        for r in range(-1, H + 1):
            blk = field[center, slot(r)].astype(F32)
            lower = jnp.where(lane == 0, pltpu.roll(west, (-(r + 1)) % W, 1), pltpu.roll(blk, 1, 1))
            upper = jnp.where(lane == W - 1, pltpu.roll(east, (W - 2 - r) % W, 1), pltpu.roll(blk, W - 1, 1))
            field[0:C, slot(r)] = lower.astype(BF16)
            field[2 * C:3 * C, slot(r)] = upper.astype(BF16)
        if LA > 3 * C:
            field[3 * C:LA, :] = jnp.zeros((LA - 3 * C, (H + 2) * W), BF16)

    def padded(field, west, east):
        gx[...] = dot(padder[...], field[...]).astype(BF16)
        for a in range(3):
            at_west = pltpu.roll(west, (a - 2) % W, 1)
            at_east = pltpu.roll(east, (H + a - 2) % W, 1)
            both = jnp.where(lane < H, at_west, jnp.where(lane < 2 * H, at_east, 0.0))
            ge[a] = dot(padder[...], both.astype(BF16)).astype(BF16)

    def mirrored(f):
        each(1, NI, lambda d: top_copy(f, fy.at[:, slot(H - 1)], d, lon(-d)).wait_recv())
        return dot(toprow[f], select[...]).astype(BF16)

    def tap_grad(w, field):
        for a in range(3):
            value = dot_nt(gx[:, W:W + N], field[:, a * W:a * W + N])
            tap[w, :, :, :, a * LA:(a + 1) * LA] = value.reshape(2, NM, PAD, LA)

    def input_grad(w):
        for a in range(3):
            wt[:, a * ROWS:(a + 1) * ROWS] = jnp.transpose(
                wfull[w].reshape(ROWS, 3 * LA)[:, a * LA:(a + 1) * LA].astype(F32)).astype(BF16)
        step = min(2 * W, N)
        for n in range(0, N, step):
            rhs = jnp.concatenate([gx[:, (2 - a) * W + n:(2 - a) * W + n + step] for a in range(3)], axis=0)
            qs[:, n:n + step] = dot(wt[...], rhs)
        qe[...] = dot(wt[...], jnp.concatenate([ge[a] for a in range(3)], axis=0))

        @pl.when(top)
        def _():
            fold = dot(wt[:, 2 * ROWS:3 * ROWS], mcat[...])
            for b in range(3):
                qs[C:2 * C, N - W:N] += fold[b * C:(b + 1) * C, b * W:(b + 1) * W]

        first, last = qe[0:C, :], qe[2 * C:3 * C, :]
        result = []
        for r in range(H):
            at = slice(r * W, (r + 1) * W)
            left = jnp.where(lane == W - 1, pltpu.roll(first, (W - 1 - H - r) % W, 1),
                             pltpu.roll(qs[0:C, at], W - 1, 1))
            right = jnp.where(lane == 0, pltpu.roll(last, (-r) % W, 1), pltpu.roll(qs[2 * C:3 * C, at], 1, 1))
            result.append(qs[C:2 * C, at] + left + right)
        return result

    def pair_copy(w, n, mine):
        return rcopy(tap.at[w, 1 - k, n], tap_in.at[w, n], r0_s.at[w, n], r0_r.at[w, n], j + 1 - 2 * k, i)

    def chip_copy(w, d, other):
        return rcopy(part.at[w, mate(d)], part_in.at[w, m if other is None else other],
                     r1_s.at[w, d], r1_r.at[w, d], 2 * mate(d) + k, i)

    def lon_copy(w, d, other):
        return rcopy(small.at[w, lon(d)], small_in.at[w, i if other is None else other],
                     r2_s.at[w, d], r2_r.at[w, d], j, lon(d))

    def sum_start(w):
        each(1, NM, lambda d: pair_copy(w, mate(d), True).start())
        pair_copy(w, m, True).start()

    def sum_chips(w):
        def step(d):
            n = mate(d)
            pair_copy(w, n, False).wait_recv()
            part[w, n] = (tap[w, k, n] + tap_in[w, n]).astype(SUM_TYPE)
            chip_copy(w, d, None).start()

        each(1, NM, step)
        pair_copy(w, m, False).wait_recv()

    def sum_lon(w):
        total = tap[w, k, m] + tap_in[w, m]
        for d in range(1, NM):
            chip_copy(w, d, mate(-d)).wait_recv()
            total = total + part_in[w, mate(-d)].astype(F32)
        slane = lax.broadcasted_iota(jnp.int32, (PAD, W), 1)
        sources = [total[:, t * W:(t + 1) * W] for t in range(3 * LA // W)]
        for s in range(NI):
            tiles = [jnp.zeros((PAD, W), F32)]
            for a in range(3):
                for b in range(3):
                    put_wide(tiles, slane, sources, a * LA + b * C + s * CI, CI, (3 * a + b) * CI)
            small[w, s] = tiles[0]
        small_in[w, i] = small[w, i]
        each(1, NI, lambda d: lon_copy(w, d, None).start())

    def sum_end(w, ref):
        each(1, NI, lambda d: lon_copy(w, d, lon(-d)).wait_recv())
        total = small_in[w, 0]
        for s in range(1, NI):
            total = total + small_in[w, s]
        total = total * cfg["factor"]
        for a in range(3):
            for b in range(3):
                n = 3 * a + b
                moved = pltpu.roll(total, (-n * CI) % W, 1) if n else total
                ref[a, b] = moved[:CJ, :CI]

    for copy in early:
        copy.wait_recv()
    clear_ends(fy)
    clear_ends(sa.at[center])
    clear_ends(sx.at[center])
    west, east = columns(0, 0)
    padded(fy, west, east)
    west, east = columns(0, 2 * H)
    shifted(sa, west, east)
    pass_on(1)

    tap_grad(1, sa)

    @pl.when(top)
    def _():
        mcat[...] = dot(padder[...], mirrored(0)).astype(BF16)
        act = sa[center, slot(H - 1)]
        for b in range(3):
            place = lax.broadcasted_iota(jnp.int32, (C, LA), 1) == (
                lax.broadcasted_iota(jnp.int32, (C, LA), 0) + b * C)
            spread = lax.dot_general(act, jnp.where(place, 1.0, 0.0).astype(BF16), (((0,), (0,)), ((), ())),
                                     preferred_element_type=F32).astype(BF16)
            value = dot(mcat[:, b * W:(b + 1) * W], spread)
            tap[1, :, :, :, 2 * LA:3 * LA] += value.reshape(2, NM, PAD, LA)

    sum_start(1)
    west, east = columns(0, 4 * H)
    shifted(sx, west, east)

    have_weights(1)
    grad_act = input_grad(1)
    packed = jnp.zeros((C, W), F32)
    for r in range(H):
        value = (grad_act[r] * ocean(r) * slope[:, r * W:(r + 1) * W]).astype(BF16)
        fh[:, slot(r)] = value
        packed = add_edges(packed, r, value.astype(F32), 0)
    edge[1] = packed.astype(BF16)
    late = halo_copies(1, (fh,))
    for copy in late:
        copy.start()
    send_top(2, fh.at[:, slot(H - 1)])

    @pl.when(top)
    def _():
        north = mirrored(1)
        for b in range(3):
            sx[b * C:(b + 1) * C, slot(H)] = north[:, b * W:(b + 1) * W]

    gx[:, W:W + N] = dot(padder[...], fh[:, W:W + N]).astype(BF16)
    tap_grad(0, sx)
    sum_start(0)
    sum_chips(1)
    pass_on(0)
    sum_chips(0)
    sum_lon(1)

    for copy in late:
        copy.wait_recv()
    clear_ends(fh)
    west, east = columns(1, 0)
    padded(fh, west, east)
    have_weights(0)

    @pl.when(top)
    def _():
        mcat[...] = dot(padder[...], mirrored(2)).astype(BF16)

    result = input_grad(0)
    cells[...] = g_ref[...].astype(F32).reshape(C * H, W)
    for r in range(H):
        at = pl.ds(r, C, stride=H)
        out_ref[at, :] = cells[at, :] + result[r]

    sum_end(1, second_ref)
    sum_lon(0)
    sum_end(0, first_ref)

    each(1, NI, lambda d: tile_copy(d, None).wait_send())
    for copy in early + late:
        copy.wait_send()
    for w in range(2):
        own_forward(w, True).wait_send()
        each(1, NM, lambda d: slab_copy(w, d, None).wait_send())
        each(1, NM, lambda d: forward_copy(w, d, True).wait_send())
        each(0, NM, lambda n: pair_copy(w, n, True).wait_send())
        each(1, NM, lambda d: chip_copy(w, d, None).wait_send())
        each(1, NI, lambda d: lon_copy(w, d, None).wait_send())

    @pl.when(top)
    def _():
        for f in range(3):
            each(1, NI, lambda d: top_copy(f, fy.at[:, slot(H - 1)], d, None).wait_send())


def body(x_codes, x_scale, h_codes, h_scale, grad_out, land, partner, w_first, w_second):
    C, H, W = x_codes.shape
    NJ, NI = lax.axis_size("lat"), lax.axis_size("lon")
    CJ, CI, NM = C // NJ, C // NI, NJ // 2
    LA, ROWS, N = up(3 * C, LANES), NJ * PAD, H * W
    cfg = {"C": C, "H": H, "NJ": NJ, "NI": NI, "factor": 1.0 / math.sqrt(NJ * H * NI * W)}
    taps = jnp.stack([w_first, w_second]).reshape(2, 9, CJ, CI).transpose(0, 2, 1, 3).reshape(2, CJ, 9 * CI)
    taps = jnp.pad(taps, ((0, 0), (0, PAD - CJ), (0, LANES - 9 * CI))).reshape(2 * PAD, LANES)
    sem = pltpu.SemaphoreType.DMA
    vm = pltpu.VMEM
    scratch = [
        vm((C * H, W), F32),
        vm((C, N), F32),
        vm((NI, 2 * PAD, LANES), BF16),
        vm((2, PAD, 3 * LA), BF16),
        vm((2, 2, NM, PAD, 3 * LA), BF16),
        vm((LA, 3 * ROWS), BF16),
        vm((C, N + 2 * W), BF16),
        vm((C, N + 2 * W), BF16),
        vm((LA, N + 2 * W), BF16),
        vm((LA, N + 2 * W), BF16),
        vm((ROWS, N + 2 * W), BF16),
        vm((3, ROWS, W), BF16),
        vm((2, C, W), BF16),
        vm((2, 6, C, W), BF16),
        vm((3, C, NI * W), BF16),
        vm((NI * W, 3 * W), BF16),
        vm((ROWS, 3 * W), BF16),
        vm((ROWS, C), BF16),
        vm((LA, N), F32),
        vm((LA, W), F32),
        vm((2, 2, NM, PAD, 3 * LA), F32),
        vm((2, NM, PAD, 3 * LA), F32),
        vm((2, NM, PAD, 3 * LA), SUM_TYPE),
        vm((2, NM, PAD, 3 * LA), SUM_TYPE),
        vm((2, NI, PAD, LANES), F32),
        vm((2, NI, PAD, LANES), F32),
        sem((NI,)), sem((NI,)), sem((2, NM)), sem((2, NM)), sem((2, NM)), sem((2, NM)),
        sem((2, 12)), sem((2, 12)), sem((3, NI)), sem((3, NI)),
        sem((2, NM)), sem((2, NM)), sem((2, NM)), sem((2, NM)), sem((2, NI)), sem((2, NI)),
    ]
    grad_in, first, second = pl.pallas_call(
        functools.partial(kernel, cfg),
        out_shape=(
            jax.ShapeDtypeStruct((C * H, W), F32),
            jax.ShapeDtypeStruct((3, 3, CJ, CI), F32),
            jax.ShapeDtypeStruct((3, 3, CJ, CI), F32),
        ),
        in_specs=[pl.BlockSpec(memory_space=vm)] * 8,
        out_specs=[pl.BlockSpec(memory_space=vm)] * 3,
        scratch_shapes=scratch,
        compiler_params=pltpu.CompilerParams(
            collective_id=0, has_side_effects=True, vmem_limit_bytes=56 * 1024 * 1024
        ),
    )(x_codes, x_scale, h_codes, h_scale, grad_out, land, partner.reshape(NI, W), taps)
    return (grad_in.reshape(C, H, W), first, second)


def solution(mesh):
    placed = (
        P(None, "lat", "lon"),
        P(None, "lat"),
        P(None, "lat", "lon"),
        P(None, "lat"),
        P(None, "lat", "lon"),
        P("lat", "lon"),
        P(),
        P(None, None, "lat", "lon"),
        P(None, None, "lat", "lon"),
    )
    return jax.shard_map(
        body,
        mesh=mesh,
        in_specs=placed,
        out_specs=(P(None, "lat", "lon"), P(None, None, "lat", "lon"), P(None, None, "lat", "lon")),
        check_vma=False,
    )
```

time: 712 us -> 88.2 us (0.12)
  waiting for transfers between devices: 299 us -> 0 us
  blocking collectives: 274 us -> 0 us
  Pallas kernels: 0 us -> 79.9 us
  local copies, waits for them, and re-layouts: 51.9 us -> 7.27 us
  starting transfers between devices: 39.9 us -> 0 us
  matrix products: 18.9 us -> 0 us
  between operations: 16.3 us -> 0.69 us
  other arithmetic: 10.3 us -> 0.02 us
    unnamed x4 -> x0, waiting for transfers between devices: 296 us -> none
    all_gather x8 -> x0, blocking collectives: 274 us -> none  [the longest x4 154 us: top_row(): return lax.all_gather(field[:, -1, :], 'lon', axis=1, tiled=True)]
    pallas_call x0 -> x1, Pallas kernels: none -> 79.9 us  [body(): pl.pallas_call(functools.partial(kernel, cfg), out_shape=(jax.ShapeDtypeS...]
    ppermute x16 -> x0, starting transfers between devices: 39.9 us -> none  [the longest x8 22.1 us: with_halo(): after = lax.ppermute(first, axis, down)]
    dot_general x42 -> x0, matrix products: 18.9 us -> none  [the longest x18 8.24 us: input_grad(): jnp.einsum('oc,ohw->chw', weight[ka, kb], ext[:, 2 - ka:2 - ka + height,...]
    gather x12 -> x0, local copies, waits for them, and re-layouts: 17.2 us -> none  [the longest x6 8.82 us: input_grad(): picked = jnp.take(row, (mirror - kb + 1) % ncols, axis=1)]
    all_gather x6 -> x0, local copies, waits for them, and re-layouts: 8.1 us -> none  [the longest x4 7.28 us: top_row(): return lax.all_gather(field[:, -1, :], 'lon', axis=1, tiled=True)]
    slice x11 -> x0, local copies, waits for them, and re-layouts: 8.02 us -> none  [the longest x2 4.21 us: input_grad(): weight[ka, kb]]
  transfers between devices with their start and end apart: 18 -> 0, of which waited for: 4 -> 0; matrix products, arithmetic and copies ran while one was open for 9% -> 0% of each run, Pallas kernels for 0% -> 0%
where the time goes in v1:
time: 88.2 us; the launch traced here: 87.9 us
  Pallas kernels  79.9 us (91%)
  local copies, waits for them, and re-layouts  7.27 us (8%)
    pallas_call x1, Pallas kernels, body(): pl.pallas_call(functools.partial(kernel, cfg), out_shape=(jax.ShapeDtypeS...  79.9 us
    unnamed x17, local copies, waits for them, and re-layouts  6.66 us

profile of v1, /device:TPU:6, one launch (start us, length us, event | category | flops | bytes accessed | tf_op | source)
XLA Modules:
  0.0 87.9 jit_solution(17352244706055780334)
XLA Ops:
  0.6 0.0 copy-start.1
  0.6 0.8 copy.16
  1.4 0.0 copy-done.1
  1.5 0.1 reshape.27
  1.6 0.0 copy-start.2
  1.6 0.6 pad.4.clone
  2.2 0.1 copy-done.2
  2.3 0.0 copy-start.3
  2.3 0.7 copy.20.xs_ref
  3.0 0.0 copy-done.3
  3.0 0.7 copy.21.hs_ref
  3.8 79.9 %shard_map.112 = (f32[1280,128]{1,0:T(8,128)}, f32[3,3,10,10]{3,2,1,0:T(8,128)}, f32[3,3,10,10]{3,2,1,0:T(8,128)}) custom-call(bf16[160,8,128]{2,1,0:T(8,128)(2,1)} %x_ref.1, f32[160,8]{1,0:T(8,128)} %copy.20.xs_ref, bf16[160,8,128]{2,1,0:T(8,128)(2,1)} %h_ref.1, f32[160,8]{1,0:T(8,128)} %copy.21.hs_ref, bf16[160,8,128]{2,1,0:T(8,128)(2,1)} %g_ref.1, ...), custom_call_target="tpu_custom_call" | custom-call | tf_op jit(solution)/shard_map/pallas_call | solution.py:514
  83.7 0.0 copy-start
  83.7 1.6 %copy.22 = f32[3,3,10,10]{3,1,2,0:T(4,128)} copy(f32[3,3,10,10]{3,2,1,0:T(8,128)} %get-tuple-element.13) | data formatting | bytes 7200
  85.3 0.0 copy-done
  85.3 0.6 copy.23
  86.0 2.0 %copy.28 = f32[160,8,128]{2,1,0:T(8,128)} copy(f32[160,8,128]{2,1,0:T(8,128)} %bitcast.7) | data formatting | bytes 1310720
  (3 shorter events, 0.1 us)
Async XLA Ops:
  0.6 0.8 copy-start.1
  1.6 0.7 copy-start.2
  2.3 0.7 copy-start.3
  83.7 1.6 %copy-start = (f32[3,3,10,10]{3,2,1,0:T(8,128)S(1)}, f32[3,3,10,10]{3,2,1,0:T(8,128)}, u32[]{:S(2)}) copy-start(f32[3,3,10,10]{3,2,1,0:T(8,128)} %get-tuple-element.14) | copy-start | bytes 10804

commit v2 on v1

v2 whole, which is shorter than its diff:
```python
import functools
import math

import jax
import jax.numpy as jnp
from jax import lax
from jax.experimental import pallas as pl
from jax.experimental.pallas import tpu as pltpu
from jax.sharding import PartitionSpec as P

MESH = pl.DeviceIdType.MESH
F32, BF16 = jnp.float32, jnp.bfloat16
PAD = 16
LANES = 128
SUM_TYPE = jnp.bfloat16


def up(value, unit):
    return -(-value // unit) * unit


def gelu_parts(h):
    k = math.sqrt(2.0 / math.pi)
    tanh_part = jnp.tanh(k * (h + 0.044715 * h * h * h))
    value = 0.5 * h * (1.0 + tanh_part)
    slope = 0.5 * (1.0 + tanh_part) + 0.5 * h * (1.0 - tanh_part * tanh_part) * k * (
        1.0 + 3.0 * 0.044715 * h * h
    )
    return (value, slope)


def dot(a, b):
    return lax.dot_general(a, b, (((1,), (0,)), ((), ())), preferred_element_type=F32)


def dot_nt(a, b):
    return lax.dot_general(a, b, (((1,), (1,)), ((), ())), preferred_element_type=F32)


def put(tiles, lane, source, source_lane, count, target_lane):
    shift = (target_lane - source_lane) % LANES
    moved = pltpu.roll(source, shift, 1) if shift else source
    tile, off = divmod(target_lane, LANES)
    keep = (lane >= off) & (lane < off + count)
    tiles[tile] = jnp.where(keep, moved, tiles[tile])
    over = off + count - LANES
    if over > 0:
        tiles[tile + 1] = jnp.where(lane < over, moved, tiles[tile + 1])


def put_wide(tiles, lane, sources, source_lane, count, target_lane):
    while count > 0:
        tile, off = divmod(source_lane, LANES)
        part = min(count, LANES - off)
        put(tiles, lane, sources[tile], off, part, target_lane)
        source_lane, target_lane, count = source_lane + part, target_lane + part, count - part


def kernel(
    cfg,
    x_ref, xs_ref, h_ref, hs_ref, g_ref, land_ref, partner_ref, w0_ref, w1_ref,
    out_ref, first_ref, second_ref,
    cells, slope, wtmp, wown, wtile, wrow, wfull, wt, wp, fy, fh, sa, sx, gq, edge, edge_in,
    mrow, mout, mirr, spread, qs, nat, tap, tap_in, part, part_in, tot, small, small_in,
    st1_s, st1_r, st2_s, st2_r, fw_s, fw_r, ha_s, ha_r, mi_s, mi_r, mo_s, mo_r,
    r0_s, r0_r, r1_s, r1_r, r2_s, r2_r,
):
    C, H, NJ, NI = cfg["C"], cfg["H"], cfg["NJ"], cfg["NI"]
    W = LANES
    CJ, CI, NM, NG = C // NJ, C // NI, NJ // 2, C // PAD
    LA, CL, RB = up(3 * C, LANES), up(C, LANES), up(3 * (C // NJ), PAD)
    ROWS = NJ * RB
    N = H * W
    j, i = lax.axis_index("lat"), lax.axis_index("lon")
    k, m = lax.rem(j, 2), lax.div(j, 2)
    top = j == NJ - 1
    bottom = j == 0
    worker = top & (i < NG)

    def rcopy(src, dst, ss, rs, dj, di):
        return pltpu.make_async_remote_copy(
            src_ref=src, dst_ref=dst, send_sem=ss, recv_sem=rs,
            device_id={"lat": dj, "lon": di}, device_id_type=MESH,
        )

    def each(lo, hi, fn):
        lax.fori_loop(lo, hi, lambda d, c: (fn(d), c)[1], 0)

    def lon(d):
        return lax.rem(i + d + NI, NI)

    def lat(d):
        return lax.rem(j + d + NJ, NJ)

    def mate(d):
        return lax.rem(m + d + NM, NM)

    barrier = pltpu.get_barrier_semaphore()

    def greet(dj, di):
        pl.semaphore_signal(barrier, inc=1, device_id={"lat": dj, "lon": di}, device_id_type=MESH)

    each(1, NI, lambda d: greet(j, lon(d)))
    each(1, NJ, lambda d: greet(lat(d), i))
    for dj in (1, -1):
        for di in (1, -1):
            greet(lat(dj), lon(di))

    for w, ref in ((1, w1_ref), (0, w0_ref)):
        wtmp[...] = jnp.zeros(wtmp.shape, F32)
        for a in range(3):
            block = ref[a].astype(F32)
            for b in range(3):
                wtmp[3 * a + b, 0:CJ, 0:CI] = block[:, b, :]
        value = wtmp[0]
        for n in range(1, 9):
            value = value + pltpu.roll(wtmp[n], n * CI, 1)
        wown[w] = value.astype(BF16)

    def blocks(ref):
        cells[...] = ref[...].astype(F32).reshape(C * H, W)
        return [cells[pl.ds(r, C, stride=H), :] for r in range(H)]

    def ocean(r):
        return land_ref[r:r + 1, :].astype(F32)

    def slot(r):
        return pl.ds((r + 1) * W, W)

    lane = lax.broadcasted_iota(jnp.int32, (C, W), 1)
    center = pl.ds(C, C)

    def add_edges(packed, f, r, blk):
        spots = [f * 8 + r]
        if r == H - 1:
            spots.append(32 + f)
        if r == 0:
            spots.append(48 + f)
        for spot in spots:
            packed = jnp.where(lane == spot, pltpu.roll(blk, spot, 1) if spot else blk, packed)
            packed = jnp.where(lane == 64 + spot, pltpu.roll(blk, 65 + spot, 1), packed)
        return packed

    def turn_edges(phase, packed):
        if CL > C:
            packed = jnp.concatenate([packed, jnp.zeros((CL - C, W), F32)], axis=0)
        edge[phase] = jnp.transpose(packed).astype(BF16)

    scale = jnp.transpose(xs_ref[...])
    packed = jnp.zeros((C, W), F32)
    for r, blk in enumerate(blocks(g_ref)):
        value = blk * ocean(r)
        fy[:, slot(r)] = value.astype(BF16)
        packed = add_edges(packed, 0, r, value)
    for r, blk in enumerate(blocks(x_ref)):
        x = (blk * scale[:, r:r + 1]).astype(BF16)
        sx[center, slot(r)] = x
        packed = add_edges(packed, 2, r, x.astype(F32))

    pl.semaphore_wait(barrier, NI - 1 + NJ - 1 + 4)

    def tile_copy(w, d, other):
        return rcopy(wown.at[w], wtile.at[w, i if other is None else other],
                     st1_s.at[w, d], st1_r.at[w, d], j, lon(d))

    each(1, NI, lambda d: tile_copy(1, d, None).start())
    wtile[1, i] = wown[1]

    def row_copy(f, src, d, other):
        g = lon(d) if other is None else i
        return rcopy(src.at[pl.ds(pl.multiple_of(g * PAD, PAD), PAD), slot(H - 1)],
                     mrow.at[f, i if other is None else other], mi_s.at[f, d], mi_r.at[f, d], j, lon(d))

    def turned_copy(f, d, other):
        g = i if other is None else other
        return rcopy(mout.at[f, lon(d)], mirr.at[f, pl.ds(pl.multiple_of(g * PAD, PAD), PAD)],
                     mo_s.at[f, d], mo_r.at[f, d], j, lon(d))

    def mirror_send(f, src):
        @pl.when(top)
        def _():
            def step(d):
                @pl.when(lon(d) < NG)
                def _():
                    row_copy(f, src, d, None).start()

            each(1, NI, step)

            @pl.when(i < NG)
            def _():
                mrow[f, i] = src[pl.ds(pl.multiple_of(i * PAD, PAD), PAD), slot(H - 1)]

    def mirror_turn(f, src):
        @pl.when(worker)
        def _():
            each(1, NI, lambda d: row_copy(f, src, d, lon(-d)).wait_recv())
            ncols = NI * W
            flip = (lax.broadcasted_iota(jnp.int32, (W, W), 0)
                    + lax.broadcasted_iota(jnp.int32, (W, W), 1)) == W - 1
            rev = dot(mrow[f].reshape(NI * PAD, W), jnp.where(flip, 1.0, 0.0).astype(BF16))
            tiles = [rev[(NI - 1 - v) * PAD:(NI - v) * PAD] for v in range(NI)]
            tlane = lax.broadcasted_iota(jnp.int32, (PAD, W), 1)
            where = partner_ref[pl.ds(i, 1), :] + lax.broadcasted_iota(jnp.int32, (1, W), 1) + i * W
            turn = (ncols - 1) - (where & (ncols - 1))
            turn = jnp.broadcast_to(turn, (PAD, W))

            def left(tiles, by):
                if by % W == 0:
                    return [tiles[(t + by // W) % NI] for t in range(NI)]
                moved = [pltpu.roll(tile, W - by, 1) for tile in tiles]
                return [jnp.where(tlane < W - by, moved[t], moved[(t + 1) % NI]) for t in range(NI)]

            for bit in range(ncols.bit_length() - 1):
                take = (turn & (1 << bit)) != 0
                tiles = [jnp.where(take, new, old) for new, old in zip(left(tiles, 1 << bit), tiles)]
            moved = [pltpu.roll(tile, 1, 1) for tile in tiles]
            before = [jnp.where(tlane == 0, moved[t - 1], moved[t]) for t in range(NI)]
            for b, group in enumerate((before, tiles, left(tiles, 1))):
                for t in range(NI):
                    mout[f, t, :, b * W:(b + 1) * W] = group[t].astype(BF16)
            mirr[f, pl.ds(pl.multiple_of(i * PAD, PAD), PAD), :] = mout[f, i]
            each(1, NI, lambda d: turned_copy(f, d, None).start())

    def mirror_wait(f):
        def step(d):
            @pl.when(lon(-d) < NG)
            def _():
                turned_copy(f, d, lon(-d)).wait_recv()

        each(1, NI, step)

    mirror_send(0, fy)
    mirror_send(1, sx.at[center])

    scale = jnp.transpose(hs_ref[...])
    for r, blk in enumerate(blocks(h_ref)):
        h = blk * scale[:, r:r + 1]
        value, deriv = gelu_parts(h)
        act = (ocean(r) * value).astype(BF16)
        sa[center, slot(r)] = act
        slope[:, r * W:(r + 1) * W] = deriv
        packed = add_edges(packed, 1, r, act.astype(F32))
    turn_edges(0, packed)

    def halo_copies(phase, fields):
        out = []
        for f, field in enumerate(fields):
            s = 2 * f
            out.append(rcopy(field.at[:, slot(H - 1)], field.at[:, slot(-1)],
                             ha_s.at[phase, s], ha_r.at[phase, s], lat(1), i))
            out.append(rcopy(field.at[:, slot(0)], field.at[:, slot(H)],
                             ha_s.at[phase, s + 1], ha_r.at[phase, s + 1], lat(-1), i))
        side = up(8 * len(fields), PAD)
        n = 6
        for di, base, target in ((1, 64, 0), (-1, 0, 64)):
            for dj, off, size in ((0, 0, side), (1, 32, PAD), (-1, 48, PAD)):
                out.append(rcopy(edge.at[phase, pl.ds(base + off, size)],
                                 edge_in.at[phase, pl.ds(target + off, size)],
                                 ha_s.at[phase, n], ha_r.at[phase, n], lat(dj), lon(di)))
                n += 1
        return out

    early = halo_copies(0, (fy, sa.at[center], sx.at[center]))
    for copy in early:
        copy.start()

    at = lax.broadcasted_iota(jnp.int32, (ROWS, 1), 0)
    half, rest = lax.div(at, NM * RB), lax.rem(at, NM * RB)
    own = lax.rem(rest, RB)
    line = lax.div(own, CJ)
    target = line * C + (2 * lax.div(rest, RB) + half) * CJ + own - line * CJ
    target = jnp.where(own < 3 * CJ, target, -1)
    spread[...] = jnp.where(lax.broadcasted_iota(jnp.int32, (ROWS, 3 * C), 1) == target, 1.0, 0.0).astype(BF16)

    def make_slab(w):
        each(1, NI, lambda d: tile_copy(w, d, lon(-d)).wait_recv())
        wlane = lax.broadcasted_iota(jnp.int32, (PAD, W), 1)
        tot[...] = jnp.zeros(tot.shape, F32)
        pieces = [wtile[w, s].astype(F32) for s in range(NI)]
        for a in range(3):
            tiles = [jnp.zeros((PAD, W), F32) for _ in range(LA // W)]
            for s in range(NI):
                for b in range(3):
                    put(tiles, wlane, pieces[s], (3 * a + b) * CI, CI, b * C + s * CI)
            for t, value in enumerate(tiles):
                tot[a * CJ:(a + 1) * CJ, t * W:(t + 1) * W] = value[:CJ]
        wrow[w] = tot[0:RB].astype(BF16)

    def slab_copy(w, d, other):
        return rcopy(wrow.at[w], wfull.at[w, k, m if other is None else other],
                     st2_s.at[w, d], st2_r.at[w, d], 2 * mate(d) + k, i)

    def forward_copy(w, d, mine):
        n = mate(-d)
        return rcopy(wfull.at[w, k, n], wfull.at[w, k if mine else 1 - k, n],
                     fw_s.at[w, d], fw_r.at[w, d], j + 1 - 2 * k, i)

    def own_forward(w, mine):
        return rcopy(wrow.at[w], wfull.at[w, k if mine else 1 - k, m], fw_s.at[w, 0], fw_r.at[w, 0],
                     j + 1 - 2 * k, i)

    def send_slab(w):
        each(1, NM, lambda d: slab_copy(w, d, None).start())
        own_forward(w, True).start()
        wfull[w, k, m] = wrow[w]

    def pass_on(w):
        def step(d):
            slab_copy(w, d, mate(-d)).wait_recv()
            forward_copy(w, d, True).start()

        each(1, NM, step)

    def have_weights(w):
        own_forward(w, False).wait_recv()
        each(1, NM, lambda d: forward_copy(w, d, False).wait_recv())
        wt[...] = jnp.transpose(wfull[w].reshape(ROWS, LA).astype(F32)).astype(BF16)

    def columns(got, f):
        result = []
        for base in (0, 64):
            start = base + f * 8
            value = jnp.where((lane >= 1) & (lane <= H), pltpu.roll(got, (1 - start) % W, 1), 0.0)
            lower = pltpu.roll(got, (-(base + 32 + f)) % W, 1)
            upper = pltpu.roll(got, (H + 1 - (base + 48 + f)) % W, 1)
            value = jnp.where((lane == 0) & jnp.logical_not(bottom), lower, value)
            value = jnp.where((lane == H + 1) & jnp.logical_not(top), upper, value)
            result.append(value)
        return result

    def turned_edges(phase):
        return jnp.transpose(edge_in[phase].astype(F32))[:C]

    def clear_ends(field):
        @pl.when(bottom)
        def _():
            field[:, slot(-1)] = jnp.zeros((C, W), BF16)

        @pl.when(top)
        def _():
            field[:, slot(H)] = jnp.zeros((C, W), BF16)

    def shifted(field, west, east):
        for r in range(-1, H + 1):
            blk = field[center, slot(r)].astype(F32)
            lower = jnp.where(lane == 0, pltpu.roll(west, (-(r + 1)) % W, 1), pltpu.roll(blk, 1, 1))
            upper = jnp.where(lane == W - 1, pltpu.roll(east, (W - 2 - r) % W, 1), pltpu.roll(blk, W - 1, 1))
            field[0:C, slot(r)] = lower.astype(BF16)
            field[2 * C:3 * C, slot(r)] = upper.astype(BF16)
        if LA > 3 * C:
            field[3 * C:LA, :] = jnp.zeros((LA - 3 * C, (H + 2) * W), BF16)

    def tap_rows(field, n, size):
        return jnp.concatenate([field[:, (2 - a) * W + n:(2 - a) * W + n + size] for a in range(3)], axis=0)

    def edge_rows(west, east):
        both = []
        for a in range(3):
            at_west = pltpu.roll(west, (a - 2) % W, 1)
            at_east = pltpu.roll(east, (H + a - 2) % W, 1)
            value = jnp.where(lane < H, at_west, jnp.where(lane < 2 * H, at_east, 0.0))
            both.append(value.astype(BF16))
        return jnp.concatenate(both, axis=0)

    def fold_rows(f):
        return jnp.concatenate([jnp.zeros((2 * C, 3 * W), BF16), mirr[f]], axis=0)

    step = min(2 * W, N)

    def tap_grad(w, grad, field):
        for a in range(3):
            nat[a] = dot_nt(grad[:, W:W + N], field[:, a * W:a * W + N])

    def tap_store(w):
        for a in range(3):
            for jj in range(NJ):
                tap[w, jj % 2, jj // 2, a * CJ:(a + 1) * CJ, :] = nat[a, jj * CJ:(jj + 1) * CJ, :]

    def add_fold(fold):
        for b in range(3):
            qs[C:2 * C, N - W:N] += fold[b * C:(b + 1) * C, b * W:(b + 1) * W]

    def shift_sum():
        first, last = qs[0:C, N:N + W], qs[2 * C:3 * C, N:N + W]
        result = []
        for r in range(H):
            at = slice(r * W, (r + 1) * W)
            left = jnp.where(lane == W - 1, pltpu.roll(first, (W - 1 - H - r) % W, 1),
                             pltpu.roll(qs[0:C, at], W - 1, 1))
            right = jnp.where(lane == 0, pltpu.roll(last, (-r) % W, 1), pltpu.roll(qs[2 * C:3 * C, at], 1, 1))
            result.append(qs[C:2 * C, at] + left + right)
        return result

    def pair_copy(w, n, mine):
        return rcopy(tap.at[w, 1 - k, n], tap_in.at[w, n], r0_s.at[w, n], r0_r.at[w, n], j + 1 - 2 * k, i)

    def chip_copy(w, d, other):
        return rcopy(part.at[w, mate(d)], part_in.at[w, m if other is None else other],
                     r1_s.at[w, d], r1_r.at[w, d], 2 * mate(d) + k, i)

    def lon_copy(w, d, other):
        return rcopy(small.at[w, lon(d)], small_in.at[w, i if other is None else other],
                     r2_s.at[w, d], r2_r.at[w, d], j, lon(d))

    def sum_start(w):
        each(1, NM, lambda d: pair_copy(w, mate(d), True).start())
        pair_copy(w, m, True).start()

    def sum_chips(w):
        def step(d):
            n = mate(d)
            pair_copy(w, n, False).wait_recv()
            part[w, n] = (tap[w, k, n] + tap_in[w, n]).astype(SUM_TYPE)
            chip_copy(w, d, None).start()

        each(1, NM, step)
        pair_copy(w, m, False).wait_recv()

    def sum_lon(w):
        total = tap[w, k, m] + tap_in[w, m]
        for d in range(1, NM):
            chip_copy(w, d, mate(-d)).wait_recv()
            total = total + part_in[w, mate(-d)].astype(F32)
        tot[0:RB] = total
        slane = lax.broadcasted_iota(jnp.int32, (PAD, W), 1)
        sources = [[tot[a * CJ:a * CJ + PAD, t * W:(t + 1) * W] for t in range(LA // W)] for a in range(3)]
        for s in range(NI):
            tiles = [jnp.zeros((PAD, W), F32)]
            for a in range(3):
                for b in range(3):
                    put_wide(tiles, slane, sources[a], b * C + s * CI, CI, (3 * a + b) * CI)
            small[w, s] = tiles[0]
        small_in[w, i] = small[w, i]
        each(1, NI, lambda d: lon_copy(w, d, None).start())

    def sum_end(w, ref):
        each(1, NI, lambda d: lon_copy(w, d, lon(-d)).wait_recv())
        total = small_in[w, 0]
        for s in range(1, NI):
            total = total + small_in[w, s]
        total = total * cfg["factor"]
        for a in range(3):
            for b in range(3):
                n = 3 * a + b
                moved = pltpu.roll(total, (-n * CI) % W, 1) if n else total
                ref[a, :, b, :] = moved[:CJ, :CI]

    make_slab(1)
    send_slab(1)
    each(1, NI, lambda d: tile_copy(0, d, None).start())
    wtile[0, i] = wown[0]
    mirror_turn(0, fy)
    mirror_turn(1, sx.at[center])
    for w in range(2):
        tap[w, :, :, 3 * CJ:RB, :] = jnp.zeros((2, NM, RB - 3 * CJ, LA), F32)

    for copy in early:
        copy.wait_recv()
    clear_ends(fy)
    clear_ends(sa.at[center])
    clear_ends(sx.at[center])
    got = turned_edges(0)
    west, east = columns(got, 0)
    for n in range(0, N, step):
        gq[:, n:n + step] = dot(spread[...], tap_rows(fy, n, step)).astype(BF16)
    gq[:, N:N + W] = dot(spread[...], edge_rows(west, east)).astype(BF16)
    pass_on(1)

    west, east = columns(got, 1)
    shifted(sa, west, east)
    west, east = columns(got, 2)
    shifted(sx, west, east)

    tap_grad(1, fy, sa)

    @pl.when(top)
    def _():
        mirror_wait(0)
        act = sa[center, slot(H - 1)]
        for b in range(3):
            place = lax.broadcasted_iota(jnp.int32, (C, LA), 1) == (
                lax.broadcasted_iota(jnp.int32, (C, LA), 0) + b * C)
            wide = lax.dot_general(act, jnp.where(place, 1.0, 0.0).astype(BF16), (((0,), (0,)), ((), ())),
                                   preferred_element_type=F32).astype(BF16)
            nat[2] += dot(mirr[0, :, b * W:(b + 1) * W], wide)
        mirror_wait(1)
        for b in range(3):
            sx[b * C:(b + 1) * C, slot(H)] = mirr[1, :, b * W:(b + 1) * W]

    tap_store(1)
    make_slab(0)

    have_weights(1)
    sum_start(1)
    send_slab(0)
    for n in range(0, N + W, step):
        size = min(step, N + W - n)
        qs[:, n:n + size] = dot(wt[...], gq[:, n:n + size])

    @pl.when(top)
    def _():
        add_fold(dot(wt[...], dot(spread[...], fold_rows(0)).astype(BF16)))

    packed = jnp.zeros((C, W), F32)
    for r, value in enumerate(shift_sum()):
        value = (value * ocean(r) * slope[:, r * W:(r + 1) * W]).astype(BF16)
        fh[:, slot(r)] = value
        packed = add_edges(packed, 0, r, value.astype(F32))
    turn_edges(1, packed)
    late = halo_copies(1, (fh,))
    for copy in late:
        copy.start()
    mirror_send(2, fh)
    sum_chips(1)

    tap_grad(0, fh, sx)
    tap_store(0)
    sum_start(0)
    pass_on(0)
    mirror_turn(2, fh)
    sum_chips(0)

    have_weights(0)
    wp[...] = dot(wt[...], spread[...]).astype(BF16)
    for copy in late:
        copy.wait_recv()
    clear_ends(fh)
    west, east = columns(turned_edges(1), 0)
    sum_lon(1)
    for n in range(0, N, step):
        qs[:, n:n + step] = dot(wp[...], tap_rows(fh, n, step))
    qs[:, N:N + W] = dot(wp[...], edge_rows(west, east))

    @pl.when(top)
    def _():
        mirror_wait(2)
        add_fold(dot(wp[...], fold_rows(2)))

    for r, value in enumerate(shift_sum()):
        out_ref[pl.ds(r, C, stride=H), :] = value

    sum_lon(0)
    sum_end(1, second_ref)
    sum_end(0, first_ref)

    for copy in early + late:
        copy.wait_send()
    for w in range(2):
        each(1, NI, lambda d: tile_copy(w, d, None).wait_send())
        own_forward(w, True).wait_send()
        each(1, NM, lambda d: slab_copy(w, d, None).wait_send())
        each(1, NM, lambda d: forward_copy(w, d, True).wait_send())
        each(0, NM, lambda n: pair_copy(w, n, True).wait_send())
        each(1, NM, lambda d: chip_copy(w, d, None).wait_send())
        each(1, NI, lambda d: lon_copy(w, d, None).wait_send())

    @pl.when(top)
    def _():
        for f in range(3):
            def sent(d):
                @pl.when(lon(d) < NG)
                def _():
                    row_copy(f, fy, d, None).wait_send()

            each(1, NI, sent)

    @pl.when(worker)
    def _():
        for f in range(3):
            each(1, NI, lambda d: turned_copy(f, d, None).wait_send())


def body(x_codes, x_scale, h_codes, h_scale, grad_out, land, partner, w_first, w_second):
    C, H, W = x_codes.shape
    NJ, NI = lax.axis_size("lat"), lax.axis_size("lon")
    CJ, CI, NM = C // NJ, C // NI, NJ // 2
    LA, CL, RB, N = up(3 * C, LANES), up(C, LANES), up(3 * CJ, PAD), H * W
    ROWS = NJ * RB
    cfg = {"C": C, "H": H, "NJ": NJ, "NI": NI, "factor": 1.0 / math.sqrt(NJ * H * NI * W)}
    sem = pltpu.SemaphoreType.DMA
    vm = pltpu.VMEM
    scratch = [
        vm((C * H, W), F32),
        vm((C, N), F32),
        vm((9, PAD, LANES), F32),
        vm((2, PAD, LANES), BF16),
        vm((2, NI, PAD, LANES), BF16),
        vm((2, RB, LA), BF16),
        vm((2, 2, NM, RB, LA), BF16),
        vm((LA, ROWS), BF16),
        vm((LA, 3 * C), BF16),
        vm((C, N + 2 * W), BF16),
        vm((C, N + 2 * W), BF16),
        vm((LA, N + 2 * W), BF16),
        vm((LA, N + 2 * W), BF16),
        vm((ROWS, N + W), BF16),
        vm((2, W, CL), BF16),
        vm((2, W, CL), BF16),
        vm((3, NI, PAD, W), BF16),
        vm((3, NI, PAD, 3 * W), BF16),
        vm((3, C, 3 * W), BF16),
        vm((ROWS, 3 * C), BF16),
        vm((LA, N + W), F32),
        vm((3, C, LA), F32),
        vm((2, 2, NM, RB, LA), F32),
        vm((2, NM, RB, LA), F32),
        vm((2, NM, RB, LA), SUM_TYPE),
        vm((2, NM, RB, LA), SUM_TYPE),
        vm((RB + PAD, LA), F32),
        vm((2, NI, PAD, LANES), F32),
        vm((2, NI, PAD, LANES), F32),
        sem((2, NI)), sem((2, NI)), sem((2, NM)), sem((2, NM)), sem((2, NM)), sem((2, NM)),
        sem((2, 12)), sem((2, 12)), sem((3, NI)), sem((3, NI)), sem((3, NI)), sem((3, NI)),
        sem((2, NM)), sem((2, NM)), sem((2, NM)), sem((2, NM)), sem((2, NI)), sem((2, NI)),
    ]
    grad_in, first, second = pl.pallas_call(
        functools.partial(kernel, cfg),
        out_shape=(
            jax.ShapeDtypeStruct((C * H, W), F32),
            jax.ShapeDtypeStruct((3, CJ, 3, CI), F32),
            jax.ShapeDtypeStruct((3, CJ, 3, CI), F32),
        ),
        in_specs=[pl.BlockSpec(memory_space=vm)] * 9,
        out_specs=[pl.BlockSpec(memory_space=vm)] * 3,
        scratch_shapes=scratch,
        compiler_params=pltpu.CompilerParams(
            collective_id=0, has_side_effects=True, vmem_limit_bytes=56 * 1024 * 1024
        ),
    )(x_codes, x_scale.T, h_codes, h_scale.T, grad_out, land, partner.reshape(NI, W),
      w_first.transpose(0, 2, 1, 3), w_second.transpose(0, 2, 1, 3))
    grad_in = grad_out.astype(F32) + grad_in.reshape(C, H, W)
    return (grad_in, first.transpose(0, 2, 1, 3), second.transpose(0, 2, 1, 3))


def solution(mesh):
    placed = (
        P(None, "lat", "lon"),
        P(None, "lat"),
        P(None, "lat", "lon"),
        P(None, "lat"),
        P(None, "lat", "lon"),
        P("lat", "lon"),
        P(),
        P(None, None, "lat", "lon"),
        P(None, None, "lat", "lon"),
    )
    return jax.shard_map(
        body,
        mesh=mesh,
        in_specs=placed,
        out_specs=(P(None, "lat", "lon"), P(None, None, "lat", "lon"), P(None, None, "lat", "lon")),
        check_vma=False,
    )
```

time: 88.2 us -> 59.3 us (0.67)
  the two profiles are of different devices: /device:TPU:6 before, /device:TPU:23 now
where the time goes in v2:
time: 59.3 us; the launch traced here: 59.1 us
  Pallas kernels  55 us (93%)
  other arithmetic  2 us (3%)
  local copies, waits for them, and re-layouts  1.48 us (2%)
  between operations  0.67 us (1%)
    pallas_call x1, Pallas kernels, body(): pl.pallas_call(functools.partial(kernel, cfg), out_shape=(jax.ShapeDtypeS...  55 us
    add x1, other arithmetic, body(): grad_in = grad_out.astype(F32) + grad_in.reshape(C, H, W)  2 us
    unnamed x8, local copies, waits for them, and re-layouts  1.48 us

profile of v2, /device:TPU:23, one launch (start us, length us, event | category | flops | bytes accessed | tf_op | source)
XLA Modules:
  0.0 59.1 jit_solution(10330762822146963190)
XLA Ops:
  0.6 0.0 copy-start
  0.6 55.0 %shard_map.112 = (f32[1280,128]{1,0:T(8,128)}, f32[3,10,3,10]{3,2,1,0:T(4,128)}, f32[3,10,3,10]{3,2,1,0:T(4,128)}) custom-call(bf16[160,8,128]{2,1,0:T(8,128)(2,1)} %x_ref.1, f32[8,160]{1,0:T(8,128)} %bitcast.13, bf16[160,8,128]{2,1,0:T(8,128)(2,1)} %h_ref.1, f32[8,160]{1,0:T(8,128)} %bitcast.14, bf16[160,8,128]{2,1,0:T(8,128)(2,1)} %g_ref.1, ...), custom_call_target="tpu_custom_call" | custom-call | tf_op jit(solution)/shard_map/pallas_call | solution.py:616
  55.6 0.0 copy-done
  55.7 0.0 copy-start.2
  55.7 2.0 %bitcast_add_fusion = f32[160,8,128]{2,1,0:T(8,128)} fusion(f32[1280,128]{1,0:T(8,128)} %get-tuple-element.6, bf16[160,8,128]{2,1,0:T(8,128)(2,1)S(1)} %copy-done), kind=kLoop, calls=%fused_computation | loop fusion | flops 327680 | bytes 1638400 | tf_op jit(solution)/shard_map/add | solution.py:631
  57.7 0.0 copy-done.2
  57.7 0.0 copy-start.1
  57.7 0.6 %copy.14 = f32[3,3,10,10]{3,1,2,0:T(4,128)} copy(f32[3,3,10,10]{3,1,2,0:T(4,128)S(1)} %bitcast.10) | data formatting | bytes 7200
  58.3 0.2 copy-done.1
  58.5 0.6 %copy.15 = f32[3,3,10,10]{3,1,2,0:T(4,128)} copy(f32[3,3,10,10]{3,1,2,0:T(4,128)S(1)} %bitcast.9) | data formatting | bytes 7200
Async XLA Ops:
  0.6 55.0 %copy-start = (bf16[160,8,128]{2,1,0:T(8,128)(2,1)S(1)}, bf16[160,8,128]{2,1,0:T(8,128)(2,1)}, u32[]{:S(2)}) copy-start(bf16[160,8,128]{2,1,0:T(8,128)(2,1)} %g_ref.1) | copy-start | bytes 983044
  55.7 2.0 %copy-start.2 = (f32[3,10,3,10]{3,2,1,0:T(4,128)S(1)}, f32[3,10,3,10]{3,2,1,0:T(4,128)}, u32[]{:S(2)}) copy-start(f32[3,10,3,10]{3,2,1,0:T(4,128)} %get-tuple-element.7) | copy-start | bytes 10804
  57.7 0.9 %copy-start.1 = (f32[3,10,3,10]{3,2,1,0:T(4,128)S(1)}, f32[3,10,3,10]{3,2,1,0:T(4,128)}, u32[]{:S(2)}) copy-start(f32[3,10,3,10]{3,2,1,0:T(4,128)} %get-tuple-element.8) | copy-start | bytes 10804

commit v3 on v2

--- a/solution.py
+++ b/solution.py
@@ -13,6 +13,8 @@
 PAD = 16
 LANES = 128
 SUM_TYPE = jnp.bfloat16
+PARTS = 4
+GRANT = 56 * 1024 * 1024
 
 
 def up(value, unit):
@@ -58,8 +60,10 @@
 
 def kernel(
     cfg,
-    x_ref, xs_ref, h_ref, hs_ref, g_ref, land_ref, partner_ref, w0_ref, w1_ref,
-    out_ref, first_ref, second_ref,
+    x_hbm, xs_hbm, h_hbm, hs_hbm, g_hbm, land_hbm, partner_hbm, w0_hbm, w1_hbm,
+    out_hbm, first_hbm, second_hbm,
+    out_ref, first_ref, second_ref, x_ref,
+    xs_ref, h_ref, hs_ref, g_ref, land_ref, partner_ref, w0_ref, w1_ref, in_s, out_s,
     cells, slope, wtmp, wown, wtile, wrow, wfull, wt, wp, fy, fh, sa, sx, gq, edge, edge_in,
     mrow, mout, mirr, spread, qs, nat, tap, tap_in, part, part_in, tot, small, small_in,
     st1_s, st1_r, st2_s, st2_r, fw_s, fw_r, ha_s, ha_r, mi_s, mi_r, mo_s, mo_r,
@@ -87,24 +91,44 @@
         lax.fori_loop(lo, hi, lambda d, c: (fn(d), c)[1], 0)
 
     def lon(d):
-        return lax.rem(i + d + NI, NI)
+        return jnp.bitwise_xor(i, d)
 
     def lat(d):
-        return lax.rem(j + d + NJ, NJ)
+        return jnp.bitwise_xor(j, d)
 
     def mate(d):
-        return lax.rem(m + d + NM, NM)
+        return jnp.bitwise_xor(m, d)
+
+    def beside(axis, place, d):
+        return lax.rem(place + d + axis, axis)
+
+    lon_order = [d for d in (9, 8, 11, 10, 7, 6, 15, 14, 5, 13, 4, 12, 3, 2, 1) if d < NI]
+    lat_order = [d for d in (12, 13, 10, 11, 14, 15, 8, 9, 4, 5, 2, 3, 6, 7, 1) if d < NJ]
+    mate_order = [d for d in (6, 5, 7, 4, 2, 1, 3) if d < NM]
 
     barrier = pltpu.get_barrier_semaphore()
 
     def greet(dj, di):
         pl.semaphore_signal(barrier, inc=1, device_id={"lat": dj, "lon": di}, device_id_type=MESH)
 
-    each(1, NI, lambda d: greet(j, lon(d)))
-    each(1, NJ, lambda d: greet(lat(d), i))
+    for d in lon_order:
+        greet(j, lon(d))
+    for d in lat_order:
+        greet(lat(d), i)
     for dj in (1, -1):
         for di in (1, -1):
-            greet(lat(dj), lon(di))
+            greet(beside(NJ, j, dj), beside(NI, i, di))
+    loads = [
+        pltpu.make_async_copy(src, dst, in_s.at[n])
+        for n, (src, dst) in enumerate((
+            (w1_hbm, w1_ref), (w0_hbm, w0_ref), (land_hbm, land_ref), (g_hbm, g_ref), (xs_hbm, xs_ref),
+            (x_hbm, x_ref), (hs_hbm, hs_ref), (h_hbm, h_ref), (partner_hbm, partner_ref)))
+    ]
+    for load in loads:
+        load.start()
+
+    loads[0].wait()
+    loads[1].wait()
 
     for w, ref in ((1, w1_ref), (0, w0_ref)):
         wtmp[...] = jnp.zeros(wtmp.shape, F32)
@@ -146,6 +170,8 @@
             packed = jnp.concatenate([packed, jnp.zeros((CL - C, W), F32)], axis=0)
         edge[phase] = jnp.transpose(packed).astype(BF16)
 
+    for load in loads[2:6]:
+        load.wait()
     scale = jnp.transpose(xs_ref[...])
     packed = jnp.zeros((C, W), F32)
     for r, blk in enumerate(blocks(g_ref)):
@@ -163,7 +189,8 @@
         return rcopy(wown.at[w], wtile.at[w, i if other is None else other],
                      st1_s.at[w, d], st1_r.at[w, d], j, lon(d))
 
-    each(1, NI, lambda d: tile_copy(1, d, None).start())
+    for d in lon_order:
+        tile_copy(1, d, None).start()
     wtile[1, i] = wown[1]
 
     def row_copy(f, src, d, other):
@@ -193,7 +220,7 @@
     def mirror_turn(f, src):
         @pl.when(worker)
         def _():
-            each(1, NI, lambda d: row_copy(f, src, d, lon(-d)).wait_recv())
+            each(1, NI, lambda d: row_copy(f, src, d, lon(d)).wait_recv())
             ncols = NI * W
             flip = (lax.broadcasted_iota(jnp.int32, (W, W), 0)
                     + lax.broadcasted_iota(jnp.int32, (W, W), 1)) == W - 1
@@ -223,15 +250,17 @@
 
     def mirror_wait(f):
         def step(d):
-            @pl.when(lon(-d) < NG)
+            @pl.when(lon(d) < NG)
             def _():
-                turned_copy(f, d, lon(-d)).wait_recv()
+                turned_copy(f, d, lon(d)).wait_recv()
 
         each(1, NI, step)
 
     mirror_send(0, fy)
     mirror_send(1, sx.at[center])
 
+    for load in loads[6:]:
+        load.wait()
     scale = jnp.transpose(hs_ref[...])
     for r, blk in enumerate(blocks(h_ref)):
         h = blk * scale[:, r:r + 1]
@@ -247,22 +276,26 @@
         for f, field in enumerate(fields):
             s = 2 * f
             out.append(rcopy(field.at[:, slot(H - 1)], field.at[:, slot(-1)],
-                             ha_s.at[phase, s], ha_r.at[phase, s], lat(1), i))
+                             ha_s.at[phase, s], ha_r.at[phase, s], beside(NJ, j, 1), i))
             out.append(rcopy(field.at[:, slot(0)], field.at[:, slot(H)],
-                             ha_s.at[phase, s + 1], ha_r.at[phase, s + 1], lat(-1), i))
+                             ha_s.at[phase, s + 1], ha_r.at[phase, s + 1], beside(NJ, j, -1), i))
         side = up(8 * len(fields), PAD)
         n = 6
         for di, base, target in ((1, 64, 0), (-1, 0, 64)):
             for dj, off, size in ((0, 0, side), (1, 32, PAD), (-1, 48, PAD)):
                 out.append(rcopy(edge.at[phase, pl.ds(base + off, size)],
                                  edge_in.at[phase, pl.ds(target + off, size)],
-                                 ha_s.at[phase, n], ha_r.at[phase, n], lat(dj), lon(di)))
+                                 ha_s.at[phase, n], ha_r.at[phase, n],
+                                 beside(NJ, j, dj), beside(NI, i, di)))
                 n += 1
         return out
 
     early = halo_copies(0, (fy, sa.at[center], sx.at[center]))
     for copy in early:
         copy.start()
+    for d in lon_order:
+        tile_copy(0, d, None).start()
+    wtile[0, i] = wown[0]
 
     at = lax.broadcasted_iota(jnp.int32, (ROWS, 1), 0)
     half, rest = lax.div(at, NM * RB), lax.rem(at, NM * RB)
@@ -273,7 +306,7 @@
     spread[...] = jnp.where(lax.broadcasted_iota(jnp.int32, (ROWS, 3 * C), 1) == target, 1.0, 0.0).astype(BF16)
 
     def make_slab(w):
-        each(1, NI, lambda d: tile_copy(w, d, lon(-d)).wait_recv())
+        each(1, NI, lambda d: tile_copy(w, d, lon(d)).wait_recv())
         wlane = lax.broadcasted_iota(jnp.int32, (PAD, W), 1)
         tot[...] = jnp.zeros(tot.shape, F32)
         pieces = [wtile[w, s].astype(F32) for s in range(NI)]
@@ -291,7 +324,7 @@
                      st2_s.at[w, d], st2_r.at[w, d], 2 * mate(d) + k, i)
 
     def forward_copy(w, d, mine):
-        n = mate(-d)
+        n = mate(d)
         return rcopy(wfull.at[w, k, n], wfull.at[w, k if mine else 1 - k, n],
                      fw_s.at[w, d], fw_r.at[w, d], j + 1 - 2 * k, i)
 
@@ -300,13 +333,14 @@
                      j + 1 - 2 * k, i)
 
     def send_slab(w):
-        each(1, NM, lambda d: slab_copy(w, d, None).start())
+        for d in mate_order:
+            slab_copy(w, d, None).start()
         own_forward(w, True).start()
         wfull[w, k, m] = wrow[w]
 
     def pass_on(w):
         def step(d):
-            slab_copy(w, d, mate(-d)).wait_recv()
+            slab_copy(w, d, mate(d)).wait_recv()
             forward_copy(w, d, True).start()
 
         each(1, NM, step)
@@ -403,7 +437,8 @@
                      r2_s.at[w, d], r2_r.at[w, d], j, lon(d))
 
     def sum_start(w):
-        each(1, NM, lambda d: pair_copy(w, mate(d), True).start())
+        for d in mate_order:
+            pair_copy(w, mate(d), True).start()
         pair_copy(w, m, True).start()
 
     def sum_chips(w):
@@ -413,14 +448,15 @@
             part[w, n] = (tap[w, k, n] + tap_in[w, n]).astype(SUM_TYPE)
             chip_copy(w, d, None).start()
 
-        each(1, NM, step)
+        for d in mate_order:
+            step(d)
         pair_copy(w, m, False).wait_recv()
 
     def sum_lon(w):
         total = tap[w, k, m] + tap_in[w, m]
         for d in range(1, NM):
-            chip_copy(w, d, mate(-d)).wait_recv()
-            total = total + part_in[w, mate(-d)].astype(F32)
+            chip_copy(w, d, mate(d)).wait_recv()
+            total = total + part_in[w, mate(d)].astype(F32)
         tot[0:RB] = total
         slane = lax.broadcasted_iota(jnp.int32, (PAD, W), 1)
         sources = [[tot[a * CJ:a * CJ + PAD, t * W:(t + 1) * W] for t in range(LA // W)] for a in range(3)]
@@ -431,10 +467,11 @@
                     put_wide(tiles, slane, sources[a], b * C + s * CI, CI, (3 * a + b) * CI)
             small[w, s] = tiles[0]
         small_in[w, i] = small[w, i]
-        each(1, NI, lambda d: lon_copy(w, d, None).start())
+        for d in lon_order:
+            lon_copy(w, d, None).start()
 
     def sum_end(w, ref):
-        each(1, NI, lambda d: lon_copy(w, d, lon(-d)).wait_recv())
+        each(1, NI, lambda d: lon_copy(w, d, lon(d)).wait_recv())
         total = small_in[w, 0]
         for s in range(1, NI):
             total = total + small_in[w, s]
@@ -447,8 +484,6 @@
 
     make_slab(1)
     send_slab(1)
-    each(1, NI, lambda d: tile_copy(0, d, None).start())
-    wtile[0, i] = wown[0]
     mirror_turn(0, fy)
     mirror_turn(1, sx.at[center])
     for w in range(2):
@@ -464,14 +499,14 @@
     for n in range(0, N, step):
         gq[:, n:n + step] = dot(spread[...], tap_rows(fy, n, step)).astype(BF16)
     gq[:, N:N + W] = dot(spread[...], edge_rows(west, east)).astype(BF16)
-    pass_on(1)
-
     west, east = columns(got, 1)
     shifted(sa, west, east)
     west, east = columns(got, 2)
     shifted(sx, west, east)
-
     tap_grad(1, fy, sa)
+    pass_on(1)
+    make_slab(0)
+    send_slab(0)
 
     @pl.when(top)
     def _():
@@ -488,11 +523,8 @@
             sx[b * C:(b + 1) * C, slot(H)] = mirr[1, :, b * W:(b + 1) * W]
 
     tap_store(1)
-    make_slab(0)
-
+    sum_start(1)
     have_weights(1)
-    sum_start(1)
-    send_slab(0)
     for n in range(0, N + W, step):
         size = min(step, N + W - n)
         qs[:, n:n + size] = dot(wt[...], gq[:, n:n + size])
@@ -501,47 +533,53 @@
     def _():
         add_fold(dot(wt[...], dot(spread[...], fold_rows(0)).astype(BF16)))
 
+    for r, value in enumerate(shift_sum()):
+        fh[:, slot(r)] = (value * ocean(r) * slope[:, r * W:(r + 1) * W]).astype(BF16)
+
+    tap_grad(0, fh, sx)
+    tap_store(0)
+    sum_start(0)
+    sum_chips(1)
+
     packed = jnp.zeros((C, W), F32)
-    for r, value in enumerate(shift_sum()):
-        value = (value * ocean(r) * slope[:, r * W:(r + 1) * W]).astype(BF16)
-        fh[:, slot(r)] = value
-        packed = add_edges(packed, 0, r, value.astype(F32))
+    for r in range(H):
+        packed = add_edges(packed, 0, r, fh[:, slot(r)].astype(F32))
     turn_edges(1, packed)
     late = halo_copies(1, (fh,))
     for copy in late:
         copy.start()
     mirror_send(2, fh)
-    sum_chips(1)
-
-    tap_grad(0, fh, sx)
-    tap_store(0)
-    sum_start(0)
+    sum_chips(0)
+
     pass_on(0)
     mirror_turn(2, fh)
-    sum_chips(0)
-
     have_weights(0)
     wp[...] = dot(wt[...], spread[...]).astype(BF16)
     for copy in late:
         copy.wait_recv()
     clear_ends(fh)
     west, east = columns(turned_edges(1), 0)
-    sum_lon(1)
     for n in range(0, N, step):
         qs[:, n:n + step] = dot(wp[...], tap_rows(fh, n, step))
     qs[:, N:N + W] = dot(wp[...], edge_rows(west, east))
+
+    sum_lon(1)
+    sum_lon(0)
 
     @pl.when(top)
     def _():
         mirror_wait(2)
         add_fold(dot(wp[...], fold_rows(2)))
 
+    cells[...] = g_ref[...].astype(F32).reshape(C * H, W)
     for r, value in enumerate(shift_sum()):
-        out_ref[pl.ds(r, C, stride=H), :] = value
-
-    sum_lon(0)
-    sum_end(1, second_ref)
-    sum_end(0, first_ref)
+        at = pl.ds(r, C, stride=H)
+        out_ref[at, :] = cells[at, :] + value
+    results = [
+        pltpu.make_async_copy(src, dst, out_s.at[n])
+        for n, (src, dst) in enumerate(((out_ref, out_hbm), (second_ref, second_hbm), (first_ref, first_hbm)))
+    ]
+    results[0].start()
 
     for copy in early + late:
         copy.wait_send()
@@ -552,7 +590,6 @@
         each(1, NM, lambda d: forward_copy(w, d, True).wait_send())
         each(0, NM, lambda n: pair_copy(w, n, True).wait_send())
         each(1, NM, lambda d: chip_copy(w, d, None).wait_send())
-        each(1, NI, lambda d: lon_copy(w, d, None).wait_send())
 
     @pl.when(top)
     def _():
@@ -568,6 +605,31 @@
     def _():
         for f in range(3):
             each(1, NI, lambda d: turned_copy(f, d, None).wait_send())
+
+    sum_end(1, second_ref)
+    results[1].start()
+    sum_end(0, first_ref)
+    results[2].start()
+    for w in range(2):
+        each(1, NI, lambda d: lon_copy(w, d, None).wait_send())
+    for result in results:
+        result.wait()
+
+
+def hand_over(out_in, first_in, second_in, out_ref, first_ref, second_ref, out_mid, first_mid, second_mid, came, went):
+    size = out_in.shape[0] // PARTS
+    ways = [(out_in.at[pl.ds(n * size, size)], out_mid.at[pl.ds(n * size, size)], out_ref.at[pl.ds(n * size, size)])
+            for n in range(PARTS)]
+    ways += [(first_in, first_mid, first_ref), (second_in, second_mid, second_ref)]
+    first = [pltpu.make_async_copy(a, b, came.at[n]) for n, (a, b, _) in enumerate(ways)]
+    then = [pltpu.make_async_copy(b, c, went.at[n]) for n, (_, b, c) in enumerate(ways)]
+    for copy in first:
+        copy.start()
+    for copy, following in zip(first, then):
+        copy.wait()
+        following.start()
+    for copy in then:
+        copy.wait()
 
 
 def body(x_codes, x_scale, h_codes, h_scale, grad_out, land, partner, w_first, w_second):
@@ -579,7 +641,15 @@
     cfg = {"C": C, "H": H, "NJ": NJ, "NI": NI, "factor": 1.0 / math.sqrt(NJ * H * NI * W)}
     sem = pltpu.SemaphoreType.DMA
     vm = pltpu.VMEM
-    scratch = [
+    args = (x_codes, x_scale.T, h_codes, h_scale.T, grad_out, land, partner.reshape(NI, W),
+            w_first.transpose(0, 2, 1, 3), w_second.transpose(0, 2, 1, 3))
+    shapes = (
+        jax.ShapeDtypeStruct((C * H, W), F32),
+        jax.ShapeDtypeStruct((3, CJ, 3, CI), F32),
+        jax.ShapeDtypeStruct((3, CJ, 3, CI), F32),
+    )
+    scratch = [vm(arg.shape, arg.dtype) for arg in shapes + args] + [
+        sem((9,)), sem((3,)),
         vm((C * H, W), F32),
         vm((C, N), F32),
         vm((9, PAD, LANES), F32),
@@ -613,23 +683,25 @@
         sem((2, 12)), sem((2, 12)), sem((3, NI)), sem((3, NI)), sem((3, NI)), sem((3, NI)),
         sem((2, NM)), sem((2, NM)), sem((2, NM)), sem((2, NM)), sem((2, NI)), sem((2, NI)),
     ]
-    grad_in, first, second = pl.pallas_call(
+    results = pl.pallas_call(
         functools.partial(kernel, cfg),
-        out_shape=(
-            jax.ShapeDtypeStruct((C * H, W), F32),
-            jax.ShapeDtypeStruct((3, CJ, 3, CI), F32),
-            jax.ShapeDtypeStruct((3, CJ, 3, CI), F32),
-        ),
-        in_specs=[pl.BlockSpec(memory_space=vm)] * 9,
-        out_specs=[pl.BlockSpec(memory_space=vm)] * 3,
+        out_shape=shapes,
+        in_specs=[pl.BlockSpec(memory_space=pl.ANY)] * 9,
+        out_specs=[pl.BlockSpec(memory_space=pl.ANY)] * 3,
         scratch_shapes=scratch,
         compiler_params=pltpu.CompilerParams(
-            collective_id=0, has_side_effects=True, vmem_limit_bytes=56 * 1024 * 1024
+            collective_id=0, has_side_effects=True, vmem_limit_bytes=GRANT
         ),
-    )(x_codes, x_scale.T, h_codes, h_scale.T, grad_out, land, partner.reshape(NI, W),
-      w_first.transpose(0, 2, 1, 3), w_second.transpose(0, 2, 1, 3))
-    grad_in = grad_out.astype(F32) + grad_in.reshape(C, H, W)
-    return (grad_in, first.transpose(0, 2, 1, 3), second.transpose(0, 2, 1, 3))
+    )(*args)
+    grad_in, first, second = pl.pallas_call(
+        hand_over,
+        out_shape=shapes,
+        in_specs=[pl.BlockSpec(memory_space=pl.ANY)] * 3,
+        out_specs=[pl.BlockSpec(memory_space=pl.ANY)] * 3,
+        scratch_shapes=[vm(arg.shape, arg.dtype) for arg in shapes] + [sem((PARTS + 2,))] * 2,
+        compiler_params=pltpu.CompilerParams(vmem_limit_bytes=GRANT),
+    )(*results)
+    return (grad_in.reshape(C, H, W), first.transpose(0, 2, 1, 3), second.transpose(0, 2, 1, 3))
 
 
 def solution(mesh):

time: 59.3 us -> 51.2 us (0.86)
  the two profiles are of different devices: /device:TPU:23 before, /device:TPU:6 now
where the time goes in v3:
time: 51.2 us; the launch traced here: 50.9 us
  Pallas kernels  50.1 us (98%)
  between operations  0.8 us (2%)
    pallas_call x1, Pallas kernels, body(): pl.pallas_call(functools.partial(kernel, cfg), out_shape=shapes, in_specs...  48.2 us
    pallas_call x1, Pallas kernels, body(): pl.pallas_call(hand_over, out_shape=shapes, in_specs=[pl.BlockSpec(memory...  1.94 us

profile of v3, /device:TPU:6, one launch (start us, length us, event | category | flops | bytes accessed | tf_op | source)
XLA Modules:
  0.0 50.9 jit_solution(411177043284817201)
XLA Ops:
  0.6 48.2 %shard_map.112 = (f32[1280,128]{1,0:T(8,128)}, f32[3,10,3,10]{3,2,1,0:T(4,128)}, f32[3,10,3,10]{3,2,1,0:T(4,128)}) custom-call(bf16[160,8,128]{2,1,0:T(8,128)(2,1)} %x_hbm.1, f32[8,160]{1,0:T(8,128)} %bitcast.10, bf16[160,8,128]{2,1,0:T(8,128)(2,1)} %h_hbm.1, f32[8,160]{1,0:T(8,128)} %bitcast.11, bf16[160,8,128]{2,1,0:T(8,128)(2,1)} %g_hbm.1, ...), custom_call_target="tpu_custom_call" | custom-call | tf_op jit(solution)/shard_map/pallas_call | solution.py:686
  48.8 1.9 %shard_map.113 = (f32[1280,128]{1,0:T(8,128)}, f32[3,10,3,10]{3,2,1,0:T(4,128)}, f32[3,10,3,10]{3,2,1,0:T(4,128)}) custom-call(f32[1280,128]{1,0:T(8,128)} %get-tuple-element.9.out_in, f32[3,10,3,10]{3,2,1,0:T(4,128)} %get-tuple-element.10.first_in, f32[3,10,3,10]{3,2,1,0:T(4,128)} %get-tuple-element.11.second_in), custom_call_target="tpu_custom_call" | custom-call | tf_op jit(solution)/shard_map/pallas_call | solution.py:696

commit v4 on v3

--- a/solution.py
+++ b/solution.py
@@ -64,10 +64,11 @@
     out_hbm, first_hbm, second_hbm,
     out_ref, first_ref, second_ref, x_ref,
     xs_ref, h_ref, hs_ref, g_ref, land_ref, partner_ref, w0_ref, w1_ref, in_s, out_s,
-    cells, slope, wtmp, wown, wtile, wrow, wfull, wt, wp, fy, fh, sa, sx, gq, edge, edge_in,
-    mrow, mout, mirr, spread, qs, nat, tap, tap_in, part, part_in, tot, small, small_in,
+    cells, slope, wtmp, wown, wtile, wrow, wfull, wt, wp, fh, act, sg, sx, gq, edge, edge_in,
+    mrow, mout, mirr, gqm, spread, qs, nat, tap, given, tap_in, part, part_in, tot, small, small_in,
+    turned, tapz, givenz, tapz_in, partz, partz_in, smallz, smallz_in,
     st1_s, st1_r, st2_s, st2_r, fw_s, fw_r, ha_s, ha_r, mi_s, mi_r, mo_s, mo_r,
-    r0_s, r0_r, r1_s, r1_r, r2_s, r2_r,
+    r0_s, r0_r, r1_s, r1_r, r2_s, r2_r, z0_s, z0_r, z1_s, z1_r, z2_s, z2_r,
 ):
     C, H, NJ, NI = cfg["C"], cfg["H"], cfg["NJ"], cfg["NI"]
     W = LANES
@@ -128,9 +129,8 @@
         load.start()
 
     loads[0].wait()
-    loads[1].wait()
-
-    for w, ref in ((1, w1_ref), (0, w0_ref)):
+
+    def make_tile(ref):
         wtmp[...] = jnp.zeros(wtmp.shape, F32)
         for a in range(3):
             block = ref[a].astype(F32)
@@ -139,7 +139,9 @@
         value = wtmp[0]
         for n in range(1, 9):
             value = value + pltpu.roll(wtmp[n], n * CI, 1)
-        wown[w] = value.astype(BF16)
+        return value
+
+    wown[1] = make_tile(w1_ref).astype(BF16)
 
     def blocks(ref):
         cells[...] = ref[...].astype(F32).reshape(C * H, W)
@@ -153,6 +155,7 @@
 
     lane = lax.broadcasted_iota(jnp.int32, (C, W), 1)
     center = pl.ds(C, C)
+    fy = sg.at[center]
 
     def add_edges(packed, f, r, blk):
         spots = [f * 8 + r]
@@ -181,7 +184,7 @@
     for r, blk in enumerate(blocks(x_ref)):
         x = (blk * scale[:, r:r + 1]).astype(BF16)
         sx[center, slot(r)] = x
-        packed = add_edges(packed, 2, r, x.astype(F32))
+        packed = add_edges(packed, 1, r, x.astype(F32))
 
     pl.semaphore_wait(barrier, NI - 1 + NJ - 1 + 4)
 
@@ -192,40 +195,35 @@
     for d in lon_order:
         tile_copy(1, d, None).start()
     wtile[1, i] = wown[1]
-
-    def row_copy(f, src, d, other):
+    def row_copy(phase, src, d, other):
         g = lon(d) if other is None else i
         return rcopy(src.at[pl.ds(pl.multiple_of(g * PAD, PAD), PAD), slot(H - 1)],
-                     mrow.at[f, i if other is None else other], mi_s.at[f, d], mi_r.at[f, d], j, lon(d))
-
-    def turned_copy(f, d, other):
-        g = i if other is None else other
-        return rcopy(mout.at[f, lon(d)], mirr.at[f, pl.ds(pl.multiple_of(g * PAD, PAD), PAD)],
-                     mo_s.at[f, d], mo_r.at[f, d], j, lon(d))
-
-    def mirror_send(f, src):
+                     mrow.at[phase, i if other is None else other],
+                     mi_s.at[phase, d], mi_r.at[phase, d], j, lon(d))
+
+    def turned_copy(phase, d, other):
+        return rcopy(mout.at[phase, lon(d)], mirr.at[phase, i if other is None else other],
+                     mo_s.at[phase, d], mo_r.at[phase, d], j, lon(d))
+
+    def mirror_send(phase, src):
         @pl.when(top)
         def _():
-            def step(d):
+            for d in lon_order:
                 @pl.when(lon(d) < NG)
                 def _():
-                    row_copy(f, src, d, None).start()
-
-            each(1, NI, step)
+                    row_copy(phase, src, d, None).start()
 
             @pl.when(i < NG)
             def _():
-                mrow[f, i] = src[pl.ds(pl.multiple_of(i * PAD, PAD), PAD), slot(H - 1)]
-
-    def mirror_turn(f, src):
+                mrow[phase, i] = src[pl.ds(pl.multiple_of(i * PAD, PAD), PAD), slot(H - 1)]
+
+    def mirror_turn(phase, src):
         @pl.when(worker)
         def _():
-            each(1, NI, lambda d: row_copy(f, src, d, lon(d)).wait_recv())
             ncols = NI * W
             flip = (lax.broadcasted_iota(jnp.int32, (W, W), 0)
                     + lax.broadcasted_iota(jnp.int32, (W, W), 1)) == W - 1
-            rev = dot(mrow[f].reshape(NI * PAD, W), jnp.where(flip, 1.0, 0.0).astype(BF16))
-            tiles = [rev[(NI - 1 - v) * PAD:(NI - v) * PAD] for v in range(NI)]
+            flip = jnp.where(flip, 1.0, 0.0).astype(BF16)
             tlane = lax.broadcasted_iota(jnp.int32, (PAD, W), 1)
             where = partner_ref[pl.ds(i, 1), :] + lax.broadcasted_iota(jnp.int32, (1, W), 1) + i * W
             turn = (ncols - 1) - (where & (ncols - 1))
@@ -237,27 +235,38 @@
                 moved = [pltpu.roll(tile, W - by, 1) for tile in tiles]
                 return [jnp.where(tlane < W - by, moved[t], moved[(t + 1) % NI]) for t in range(NI)]
 
+            each(1, NI, lambda d: row_copy(phase, src, d, lon(d)).wait_recv())
+            rev = dot(mrow[phase].reshape(NI * PAD, W), flip)
+            tiles = [rev[(NI - 1 - v) * PAD:(NI - v) * PAD] for v in range(NI)]
             for bit in range(ncols.bit_length() - 1):
                 take = (turn & (1 << bit)) != 0
                 tiles = [jnp.where(take, new, old) for new, old in zip(left(tiles, 1 << bit), tiles)]
-            moved = [pltpu.roll(tile, 1, 1) for tile in tiles]
-            before = [jnp.where(tlane == 0, moved[t - 1], moved[t]) for t in range(NI)]
-            for b, group in enumerate((before, tiles, left(tiles, 1))):
-                for t in range(NI):
-                    mout[f, t, :, b * W:(b + 1) * W] = group[t].astype(BF16)
-            mirr[f, pl.ds(pl.multiple_of(i * PAD, PAD), PAD), :] = mout[f, i]
-            each(1, NI, lambda d: turned_copy(f, d, None).start())
-
-    def mirror_wait(f):
+            for t in range(NI):
+                before, after = pltpu.roll(tiles[t - 1], 1, 1), pltpu.roll(tiles[(t + 1) % NI], 1, 1)
+                mout[phase, t, 0] = tiles[t].astype(BF16)
+                mout[phase, t, 1] = jnp.where(tlane == 0, before, after).astype(BF16)
+            mirr[phase, i] = mout[phase, i]
+            for d in lon_order:
+                turned_copy(phase, d, None).start()
+
+    def mirror_wait(phase):
         def step(d):
             @pl.when(lon(d) < NG)
             def _():
-                turned_copy(f, d, lon(d)).wait_recv()
+                turned_copy(phase, d, lon(d)).wait_recv()
 
         each(1, NI, step)
 
+    def mirrored(phase):
+        block = mirr[phase, :, 0].reshape(C, W).astype(F32)
+        edges = mirr[phase, :, 1].reshape(C, W).astype(F32)
+        before = jnp.where(lane == 0, edges, pltpu.roll(block, 1, 1))
+        after = jnp.where(lane == W - 1, pltpu.roll(edges, W - 2, 1), pltpu.roll(block, W - 1, 1))
+        return jnp.concatenate([before, block, after], axis=1).astype(BF16)
+
     mirror_send(0, fy)
-    mirror_send(1, sx.at[center])
+    loads[1].wait()
+    wown[0] = make_tile(w0_ref).astype(BF16)
 
     for load in loads[6:]:
         load.wait()
@@ -265,38 +274,53 @@
     for r, blk in enumerate(blocks(h_ref)):
         h = blk * scale[:, r:r + 1]
         value, deriv = gelu_parts(h)
-        act = (ocean(r) * value).astype(BF16)
-        sa[center, slot(r)] = act
+        act[:, r * W:(r + 1) * W] = (ocean(r) * value).astype(BF16)
         slope[:, r * W:(r + 1) * W] = deriv
-        packed = add_edges(packed, 1, r, act.astype(F32))
     turn_edges(0, packed)
 
     def halo_copies(phase, fields):
+        north, south = jnp.logical_not(top), jnp.logical_not(bottom)
         out = []
         for f, field in enumerate(fields):
             s = 2 * f
-            out.append(rcopy(field.at[:, slot(H - 1)], field.at[:, slot(-1)],
-                             ha_s.at[phase, s], ha_r.at[phase, s], beside(NJ, j, 1), i))
-            out.append(rcopy(field.at[:, slot(0)], field.at[:, slot(H)],
-                             ha_s.at[phase, s + 1], ha_r.at[phase, s + 1], beside(NJ, j, -1), i))
+            out.append((rcopy(field.at[:, slot(H - 1)], field.at[:, slot(-1)],
+                              ha_s.at[phase, s], ha_r.at[phase, s], beside(NJ, j, 1), i), north, south))
+            out.append((rcopy(field.at[:, slot(0)], field.at[:, slot(H)],
+                              ha_s.at[phase, s + 1], ha_r.at[phase, s + 1], beside(NJ, j, -1), i), south, north))
         side = up(8 * len(fields), PAD)
         n = 6
         for di, base, target in ((1, 64, 0), (-1, 0, 64)):
             for dj, off, size in ((0, 0, side), (1, 32, PAD), (-1, 48, PAD)):
-                out.append(rcopy(edge.at[phase, pl.ds(base + off, size)],
-                                 edge_in.at[phase, pl.ds(target + off, size)],
-                                 ha_s.at[phase, n], ha_r.at[phase, n],
-                                 beside(NJ, j, dj), beside(NI, i, di)))
+                sent, comes = {0: (None, None), 1: (north, south), -1: (south, north)}[dj]
+                out.append((rcopy(edge.at[phase, pl.ds(base + off, size)],
+                                  edge_in.at[phase, pl.ds(target + off, size)],
+                                  ha_s.at[phase, n], ha_r.at[phase, n],
+                                  beside(NJ, j, dj), beside(NI, i, di)), sent, comes))
                 n += 1
         return out
 
-    early = halo_copies(0, (fy, sa.at[center], sx.at[center]))
-    for copy in early:
-        copy.start()
-    for d in lon_order:
-        tile_copy(0, d, None).start()
-    wtile[0, i] = wown[0]
-
+    def only(condition, fn):
+        if condition is None:
+            fn()
+        else:
+            pl.when(condition)(fn)
+
+    def halo_start(copies):
+        for copy, sent, _ in copies:
+            only(sent, copy.start)
+
+    def halo_wait(copies):
+        for copy, _, comes in copies:
+            only(comes, copy.wait_recv)
+
+    def halo_sent(copies):
+        for copy, sent, _ in copies:
+            only(sent, copy.wait_send)
+
+    early = halo_copies(0, (fy, sx.at[center]))
+    halo_start(early)
+
+    mirror_send(2, sx.at[center])
     at = lax.broadcasted_iota(jnp.int32, (ROWS, 1), 0)
     half, rest = lax.div(at, NM * RB), lax.rem(at, NM * RB)
     own = lax.rem(rest, RB)
@@ -396,19 +420,24 @@
             both.append(value.astype(BF16))
         return jnp.concatenate(both, axis=0)
 
-    def fold_rows(f):
-        return jnp.concatenate([jnp.zeros((2 * C, 3 * W), BF16), mirr[f]], axis=0)
+    def fold_rows(mirror):
+        return jnp.concatenate([jnp.zeros((2 * C, 3 * W), BF16), mirror], axis=0)
 
     step = min(2 * W, N)
 
-    def tap_grad(w, grad, field):
+    def tap_grad(grad, field):
         for a in range(3):
-            nat[a] = dot_nt(grad[:, W:W + N], field[:, a * W:a * W + N])
-
-    def tap_store(w):
+            nat[a * C:(a + 1) * C, :] = dot_nt(grad[:, W:W + N], field[:, a * W:a * W + N])
+
+    def tap_store():
         for a in range(3):
             for jj in range(NJ):
-                tap[w, jj % 2, jj // 2, a * CJ:(a + 1) * CJ, :] = nat[a, jj * CJ:(jj + 1) * CJ, :]
+                tap[jj % 2, jj // 2, a * CJ:(a + 1) * CJ, :] = nat[a * C + jj * CJ:a * C + (jj + 1) * CJ, :]
+
+    def side_store():
+        for a in range(3):
+            for s in range(NI):
+                tapz[s, a * CI:(a + 1) * CI, :] = nat[a * C + s * CI:a * C + (s + 1) * CI, :]
 
     def add_fold(fold):
         for b in range(3):
@@ -425,38 +454,35 @@
             result.append(qs[C:2 * C, at] + left + right)
         return result
 
-    def pair_copy(w, n, mine):
-        return rcopy(tap.at[w, 1 - k, n], tap_in.at[w, n], r0_s.at[w, n], r0_r.at[w, n], j + 1 - 2 * k, i)
-
-    def chip_copy(w, d, other):
-        return rcopy(part.at[w, mate(d)], part_in.at[w, m if other is None else other],
-                     r1_s.at[w, d], r1_r.at[w, d], 2 * mate(d) + k, i)
-
-    def lon_copy(w, d, other):
-        return rcopy(small.at[w, lon(d)], small_in.at[w, i if other is None else other],
-                     r2_s.at[w, d], r2_r.at[w, d], j, lon(d))
-
-    def sum_start(w):
+    def pair_copy(n):
+        return rcopy(given.at[n], tap_in.at[n], r0_s.at[n], r0_r.at[n], j + 1 - 2 * k, i)
+
+    def chip_copy(d, other):
+        return rcopy(part.at[mate(d)], part_in.at[m if other is None else other],
+                     r1_s.at[d], r1_r.at[d], 2 * mate(d) + k, i)
+
+    def lon_copy(d, other):
+        return rcopy(small.at[lon(d)], small_in.at[i if other is None else other], r2_s.at[d], r2_r.at[d], j, lon(d))
+
+    def sum_start():
+        given[...] = tap[1 - k].astype(SUM_TYPE)
         for d in mate_order:
-            pair_copy(w, mate(d), True).start()
-        pair_copy(w, m, True).start()
-
-    def sum_chips(w):
-        def step(d):
+            pair_copy(mate(d)).start()
+        pair_copy(m).start()
+
+    def sum_chips():
+        for d in mate_order:
             n = mate(d)
-            pair_copy(w, n, False).wait_recv()
-            part[w, n] = (tap[w, k, n] + tap_in[w, n]).astype(SUM_TYPE)
-            chip_copy(w, d, None).start()
-
-        for d in mate_order:
-            step(d)
-        pair_copy(w, m, False).wait_recv()
-
-    def sum_lon(w):
-        total = tap[w, k, m] + tap_in[w, m]
+            pair_copy(n).wait_recv()
+            part[n] = (tap[k, n] + tap_in[n].astype(F32)).astype(SUM_TYPE)
+            chip_copy(d, None).start()
+        pair_copy(m).wait_recv()
+
+    def sum_lon():
+        total = tap[k, m] + tap_in[m].astype(F32)
         for d in range(1, NM):
-            chip_copy(w, d, mate(d)).wait_recv()
-            total = total + part_in[w, mate(d)].astype(F32)
+            chip_copy(d, mate(d)).wait_recv()
+            total = total + part_in[mate(d)].astype(F32)
         tot[0:RB] = total
         slane = lax.broadcasted_iota(jnp.int32, (PAD, W), 1)
         sources = [[tot[a * CJ:a * CJ + PAD, t * W:(t + 1) * W] for t in range(LA // W)] for a in range(3)]
@@ -465,65 +491,118 @@
             for a in range(3):
                 for b in range(3):
                     put_wide(tiles, slane, sources[a], b * C + s * CI, CI, (3 * a + b) * CI)
-            small[w, s] = tiles[0]
-        small_in[w, i] = small[w, i]
+            small[s] = tiles[0]
+        small_in[i] = small[i]
         for d in lon_order:
-            lon_copy(w, d, None).start()
-
-    def sum_end(w, ref):
-        each(1, NI, lambda d: lon_copy(w, d, lon(d)).wait_recv())
-        total = small_in[w, 0]
+            lon_copy(d, None).start()
+
+    def sum_end():
+        each(1, NI, lambda d: lon_copy(d, lon(d)).wait_recv())
+        total = small_in[0]
         for s in range(1, NI):
-            total = total + small_in[w, s]
+            total = total + small_in[s]
         total = total * cfg["factor"]
         for a in range(3):
             for b in range(3):
                 n = 3 * a + b
                 moved = pltpu.roll(total, (-n * CI) % W, 1) if n else total
-                ref[a, :, b, :] = moved[:CJ, :CI]
+                first_ref[a, :, b, :] = moved[:CJ, :CI]
+
+    HR = RB // 2
+    mine = pl.ds(pl.multiple_of(k * HR, HR), HR)
+    others = pl.ds(pl.multiple_of((1 - k) * HR, HR), HR)
+
+    def side_pair():
+        return rcopy(givenz, tapz_in, z0_s, z0_r, j + 1 - 2 * k, i)
+
+    def side_lon(d, other):
+        return rcopy(partz.at[lon(d)], partz_in.at[i if other is None else other], z1_s.at[d], z1_r.at[d], j, lon(d))
+
+    def side_lat(d, other):
+        return rcopy(smallz.at[lat(d)], smallz_in.at[j if other is None else other], z2_s.at[d], z2_r.at[d], lat(d), i)
+
+    def side_start():
+        givenz[...] = tapz[:, others].astype(SUM_TYPE)
+        side_pair().start()
+
+    def side_sum_lon():
+        side_pair().wait_recv()
+        for s in range(NI):
+            partz[s] = (tapz[s, mine] + tapz_in[s].astype(F32)).astype(SUM_TYPE)
+        for d in lon_order:
+            side_lon(d, None).start()
+
+    def side_sum_lat():
+        total = tapz[i, mine] + tapz_in[i].astype(F32)
+        for d in range(1, NI):
+            side_lon(d, lon(d)).wait_recv()
+            total = total + partz_in[lon(d)].astype(F32)
+        slane = lax.broadcasted_iota(jnp.int32, (HR, W), 1)
+        sources = [total[:, t * W:(t + 1) * W] for t in range(LA // W)]
+        for s in range(NJ):
+            tiles = [jnp.zeros((HR, W), F32)]
+            for a in range(3):
+                put_wide(tiles, slane, sources, a * C + s * CJ, CJ, a * CJ)
+            smallz[s] = tiles[0]
+        smallz_in[j] = smallz[j]
+        for d in lat_order:
+            side_lat(d, None).start()
+
+    def side_end():
+        each(1, NJ, lambda d: side_lat(d, lat(d)).wait_recv())
+        halves = []
+        for h in range(2):
+            total = smallz_in[h]
+            for s in range(h + 2, NJ, 2):
+                total = total + smallz_in[s]
+            halves.append(total)
+        total = jnp.concatenate(halves + [jnp.zeros((W - RB, W), F32)], axis=0) * cfg["factor"]
+        turned[...] = jnp.transpose(total)
+        for b in range(3):
+            block = turned[(2 - b) * CJ:(3 - b) * CJ, :]
+            for a in range(3):
+                moved = pltpu.roll(block, (-a * CI) % W, 1) if a else block
+                second_ref[a, :, b, :] = moved[:, :CI]
 
     make_slab(1)
     send_slab(1)
+    for d in lon_order:
+        tile_copy(0, d, None).start()
+    wtile[0, i] = wown[0]
     mirror_turn(0, fy)
-    mirror_turn(1, sx.at[center])
-    for w in range(2):
-        tap[w, :, :, 3 * CJ:RB, :] = jnp.zeros((2, NM, RB - 3 * CJ, LA), F32)
-
-    for copy in early:
-        copy.wait_recv()
+    tap[:, :, 3 * CJ:RB, :] = jnp.zeros((2, NM, RB - 3 * CJ, LA), F32)
+    tapz[:, 3 * CI:RB, :] = jnp.zeros((NI, RB - 3 * CI, LA), F32)
+
+    halo_wait(early)
     clear_ends(fy)
-    clear_ends(sa.at[center])
     clear_ends(sx.at[center])
     got = turned_edges(0)
     west, east = columns(got, 0)
     for n in range(0, N, step):
         gq[:, n:n + step] = dot(spread[...], tap_rows(fy, n, step)).astype(BF16)
     gq[:, N:N + W] = dot(spread[...], edge_rows(west, east)).astype(BF16)
+    mirror_turn(2, sx.at[center])
+    shifted(sg, west, east)
     west, east = columns(got, 1)
-    shifted(sa, west, east)
-    west, east = columns(got, 2)
     shifted(sx, west, east)
-    tap_grad(1, fy, sa)
+    for a in range(3):
+        nat[a * C:(a + 1) * C, :] = dot_nt(act[...], sg[:, (2 - a) * W:(2 - a) * W + N])
     pass_on(1)
     make_slab(0)
     send_slab(0)
-
+    side_store()
     @pl.when(top)
     def _():
         mirror_wait(0)
-        act = sa[center, slot(H - 1)]
-        for b in range(3):
-            place = lax.broadcasted_iota(jnp.int32, (C, LA), 1) == (
-                lax.broadcasted_iota(jnp.int32, (C, LA), 0) + b * C)
-            wide = lax.dot_general(act, jnp.where(place, 1.0, 0.0).astype(BF16), (((0,), (0,)), ((), ())),
-                                   preferred_element_type=F32).astype(BF16)
-            nat[2] += dot(mirr[0, :, b * W:(b + 1) * W], wide)
-        mirror_wait(1)
-        for b in range(3):
-            sx[b * C:(b + 1) * C, slot(H)] = mirr[1, :, b * W:(b + 1) * W]
-
-    tap_store(1)
-    sum_start(1)
+        mirror = mirrored(0)
+        stacked = jnp.concatenate([mirror[:, 2 * W:3 * W], mirror[:, W:2 * W], mirror[:, 0:W],
+                                   jnp.zeros((LA - 3 * C, W), BF16)], axis=0)
+        nat[0:C, :] = dot_nt(act[:, N - W:N], stacked)
+        for s in range(NI):
+            tapz[s, 2 * CI:3 * CI, :] += nat[s * CI:(s + 1) * CI, :]
+        gqm[...] = dot(spread[...], fold_rows(mirror)).astype(BF16)
+
+    side_start()
     have_weights(1)
     for n in range(0, N + W, step):
         size = min(step, N + W - n)
@@ -531,45 +610,47 @@
 
     @pl.when(top)
     def _():
-        add_fold(dot(wt[...], dot(spread[...], fold_rows(0)).astype(BF16)))
-
+        add_fold(dot(wt[...], gqm[...]))
+        mirror_wait(2)
+        north = mirrored(2)
+        for b in range(3):
+            sx[b * C:(b + 1) * C, slot(H)] = north[:, b * W:(b + 1) * W]
+
+    side_sum_lon()
     for r, value in enumerate(shift_sum()):
         fh[:, slot(r)] = (value * ocean(r) * slope[:, r * W:(r + 1) * W]).astype(BF16)
 
-    tap_grad(0, fh, sx)
-    tap_store(0)
-    sum_start(0)
-    sum_chips(1)
-
+    mirror_send(1, fh)
+    tap_grad(fh, sx)
+    tap_store()
+    sum_start()
     packed = jnp.zeros((C, W), F32)
     for r in range(H):
         packed = add_edges(packed, 0, r, fh[:, slot(r)].astype(F32))
     turn_edges(1, packed)
     late = halo_copies(1, (fh,))
-    for copy in late:
-        copy.start()
-    mirror_send(2, fh)
-    sum_chips(0)
+    halo_start(late)
+    sum_chips()
+
 
     pass_on(0)
-    mirror_turn(2, fh)
     have_weights(0)
     wp[...] = dot(wt[...], spread[...]).astype(BF16)
-    for copy in late:
-        copy.wait_recv()
+    mirror_turn(1, fh)
+    side_sum_lat()
+    sum_lon()
+
+    halo_wait(late)
     clear_ends(fh)
     west, east = columns(turned_edges(1), 0)
     for n in range(0, N, step):
         qs[:, n:n + step] = dot(wp[...], tap_rows(fh, n, step))
     qs[:, N:N + W] = dot(wp[...], edge_rows(west, east))
 
-    sum_lon(1)
-    sum_lon(0)
-
     @pl.when(top)
     def _():
-        mirror_wait(2)
-        add_fold(dot(wp[...], fold_rows(2)))
+        mirror_wait(1)
+        add_fold(dot(wp[...], fold_rows(mirrored(1))))
 
     cells[...] = g_ref[...].astype(F32).reshape(C * H, W)
     for r, value in enumerate(shift_sum()):
@@ -581,37 +662,38 @@
     ]
     results[0].start()
 
-    for copy in early + late:
-        copy.wait_send()
+    halo_sent(early + late)
     for w in range(2):
         each(1, NI, lambda d: tile_copy(w, d, None).wait_send())
         own_forward(w, True).wait_send()
         each(1, NM, lambda d: slab_copy(w, d, None).wait_send())
         each(1, NM, lambda d: forward_copy(w, d, True).wait_send())
-        each(0, NM, lambda n: pair_copy(w, n, True).wait_send())
-        each(1, NM, lambda d: chip_copy(w, d, None).wait_send())
+    each(0, NM, lambda n: pair_copy(n).wait_send())
+    each(1, NM, lambda d: chip_copy(d, None).wait_send())
+    side_pair().wait_send()
+    each(1, NI, lambda d: side_lon(d, None).wait_send())
 
     @pl.when(top)
     def _():
-        for f in range(3):
+        for phase in range(3):
             def sent(d):
                 @pl.when(lon(d) < NG)
                 def _():
-                    row_copy(f, fy, d, None).wait_send()
+                    row_copy(phase, fy, d, None).wait_send()
 
             each(1, NI, sent)
 
     @pl.when(worker)
     def _():
-        for f in range(3):
-            each(1, NI, lambda d: turned_copy(f, d, None).wait_send())
-
-    sum_end(1, second_ref)
+        for phase in range(3):
+            each(1, NI, lambda d: turned_copy(phase, d, None).wait_send())
+
+    side_end()
     results[1].start()
-    sum_end(0, first_ref)
+    sum_end()
     results[2].start()
-    for w in range(2):
-        each(1, NI, lambda d: lon_copy(w, d, None).wait_send())
+    each(1, NI, lambda d: lon_copy(d, None).wait_send())
+    each(1, NJ, lambda d: side_lat(d, None).wait_send())
     for result in results:
         result.wait()
 
@@ -660,28 +742,39 @@
         vm((LA, ROWS), BF16),
         vm((LA, 3 * C), BF16),
         vm((C, N + 2 * W), BF16),
-        vm((C, N + 2 * W), BF16),
+        vm((C, N), BF16),
         vm((LA, N + 2 * W), BF16),
         vm((LA, N + 2 * W), BF16),
         vm((ROWS, N + W), BF16),
         vm((2, W, CL), BF16),
         vm((2, W, CL), BF16),
         vm((3, NI, PAD, W), BF16),
-        vm((3, NI, PAD, 3 * W), BF16),
-        vm((3, C, 3 * W), BF16),
+        vm((3, NI, 2, PAD, W), BF16),
+        vm((3, C // PAD, 2, PAD, W), BF16),
+        vm((ROWS, 3 * W), BF16),
         vm((ROWS, 3 * C), BF16),
         vm((LA, N + W), F32),
-        vm((3, C, LA), F32),
-        vm((2, 2, NM, RB, LA), F32),
+        vm((3 * C, LA), F32),
         vm((2, NM, RB, LA), F32),
-        vm((2, NM, RB, LA), SUM_TYPE),
-        vm((2, NM, RB, LA), SUM_TYPE),
+        vm((NM, RB, LA), SUM_TYPE),
+        vm((NM, RB, LA), SUM_TYPE),
+        vm((NM, RB, LA), SUM_TYPE),
+        vm((NM, RB, LA), SUM_TYPE),
         vm((RB + PAD, LA), F32),
-        vm((2, NI, PAD, LANES), F32),
-        vm((2, NI, PAD, LANES), F32),
+        vm((NI, PAD, LANES), F32),
+        vm((NI, PAD, LANES), F32),
+        vm((LANES, LANES), F32),
+        vm((NI, RB, LA), F32),
+        vm((NI, RB // 2, LA), SUM_TYPE),
+        vm((NI, RB // 2, LA), SUM_TYPE),
+        vm((NI, RB // 2, LA), SUM_TYPE),
+        vm((NI, RB // 2, LA), SUM_TYPE),
+        vm((NJ, RB // 2, LANES), F32),
+        vm((NJ, RB // 2, LANES), F32),
         sem((2, NI)), sem((2, NI)), sem((2, NM)), sem((2, NM)), sem((2, NM)), sem((2, NM)),
         sem((2, 12)), sem((2, 12)), sem((3, NI)), sem((3, NI)), sem((3, NI)), sem((3, NI)),
-        sem((2, NM)), sem((2, NM)), sem((2, NM)), sem((2, NM)), sem((2, NI)), sem((2, NI)),
+        sem((NM,)), sem((NM,)), sem((NM,)), sem((NM,)), sem((NI,)), sem((NI,)),
+        sem, sem, sem((NI,)), sem((NI,)), sem((NJ,)), sem((NJ,)),
     ]
     results = pl.pallas_call(
         functools.partial(kernel, cfg),

time: 51.2 us -> 47.8 us (0.934)
  Pallas kernels: 50.1 us -> 46.5 us
    pallas_call x1, Pallas kernels: 48.2 us -> 44.6 us  [body(): pl.pallas_call(functools.partial(kernel, cfg), out_shape=shapes, in_specs...]
where the time goes in v4:
time: 47.8 us; the launch traced here: 47.3 us
  Pallas kernels  46.5 us (97%)
  between operations  0.8 us (2%)
    pallas_call x1, Pallas kernels, body(): pl.pallas_call(functools.partial(kernel, cfg), out_shape=shapes, in_specs...  44.6 us
    pallas_call x1, Pallas kernels, body(): pl.pallas_call(hand_over, out_shape=shapes, in_specs=[pl.BlockSpec(memory...  1.94 us

profile of v4, /device:TPU:6, one launch (start us, length us, event | category | flops | bytes accessed | tf_op | source)
XLA Modules:
  0.0 47.3 jit_solution(2792773062776844542)
XLA Ops:
  0.6 44.6 %shard_map.112 = (f32[1280,128]{1,0:T(8,128)}, f32[3,10,3,10]{3,2,1,0:T(4,128)}, f32[3,10,3,10]{3,2,1,0:T(4,128)}) custom-call(bf16[160,8,128]{2,1,0:T(8,128)(2,1)} %x_hbm.1, f32[8,160]{1,0:T(8,128)} %bitcast.10, bf16[160,8,128]{2,1,0:T(8,128)(2,1)} %h_hbm.1, f32[8,160]{1,0:T(8,128)} %bitcast.11, bf16[160,8,128]{2,1,0:T(8,128)(2,1)} %g_hbm.1, ...), custom_call_target="tpu_custom_call" | custom-call | tf_op jit(solution)/shard_map/pallas_call | solution.py:779
  45.2 1.9 %shard_map.113 = (f32[1280,128]{1,0:T(8,128)}, f32[3,10,3,10]{3,2,1,0:T(4,128)}, f32[3,10,3,10]{3,2,1,0:T(4,128)}) custom-call(f32[1280,128]{1,0:T(8,128)} %get-tuple-element.9.out_in, f32[3,10,3,10]{3,2,1,0:T(4,128)} %get-tuple-element.10.first_in, f32[3,10,3,10]{3,2,1,0:T(4,128)} %get-tuple-element.11.second_in), custom_call_target="tpu_custom_call" | custom-call | tf_op jit(solution)/shard_map/pallas_call | solution.py:789

commit v5 on v4

--- a/solution.py
+++ b/solution.py
@@ -13,7 +13,7 @@
 PAD = 16
 LANES = 128
 SUM_TYPE = jnp.bfloat16
-PARTS = 4
+PARTS = 2
 GRANT = 56 * 1024 * 1024
 
 
@@ -321,6 +321,9 @@
     halo_start(early)
 
     mirror_send(2, sx.at[center])
+    for d in lon_order:
+        tile_copy(0, d, None).start()
+    wtile[0, i] = wown[0]
     at = lax.broadcasted_iota(jnp.int32, (ROWS, 1), 0)
     half, rest = lax.div(at, NM * RB), lax.rem(at, NM * RB)
     own = lax.rem(rest, RB)
@@ -439,9 +442,11 @@
             for s in range(NI):
                 tapz[s, a * CI:(a + 1) * CI, :] = nat[a * C + s * CI:a * C + (s + 1) * CI, :]
 
-    def add_fold(fold):
-        for b in range(3):
-            qs[C:2 * C, N - W:N] += fold[b * C:(b + 1) * C, b * W:(b + 1) * W]
+    def add_fold(weight, rows):
+        share = dot(weight[0:C, :], rows[:, 0:W])
+        for b in (1, 2):
+            share = share + dot(weight[b * C:(b + 1) * C, :], rows[:, b * W:(b + 1) * W])
+        qs[C:2 * C, N - W:N] += share
 
     def shift_sum():
         first, last = qs[0:C, N:N + W], qs[2 * C:3 * C, N:N + W]
@@ -529,8 +534,12 @@
         side_pair().wait_recv()
         for s in range(NI):
             partz[s] = (tapz[s, mine] + tapz_in[s].astype(F32)).astype(SUM_TYPE)
+        side_send(1)
+
+    def side_send(odd):
         for d in lon_order:
-            side_lon(d, None).start()
+            if d % 2 == odd:
+                side_lon(d, None).start()
 
     def side_sum_lat():
         total = tapz[i, mine] + tapz_in[i].astype(F32)
@@ -566,9 +575,6 @@
 
     make_slab(1)
     send_slab(1)
-    for d in lon_order:
-        tile_copy(0, d, None).start()
-    wtile[0, i] = wown[0]
     mirror_turn(0, fy)
     tap[:, :, 3 * CJ:RB, :] = jnp.zeros((2, NM, RB - 3 * CJ, LA), F32)
     tapz[:, 3 * CI:RB, :] = jnp.zeros((NI, RB - 3 * CI, LA), F32)
@@ -587,8 +593,8 @@
     shifted(sx, west, east)
     for a in range(3):
         nat[a * C:(a + 1) * C, :] = dot_nt(act[...], sg[:, (2 - a) * W:(2 - a) * W + N])
+    make_slab(0)
     pass_on(1)
-    make_slab(0)
     send_slab(0)
     side_store()
     @pl.when(top)
@@ -608,19 +614,29 @@
         size = min(step, N + W - n)
         qs[:, n:n + size] = dot(wt[...], gq[:, n:n + size])
 
+    side_sum_lon()
+
+    @pl.when(m != NM - 1)
+    def _():
+        side_send(0)
+
     @pl.when(top)
     def _():
-        add_fold(dot(wt[...], gqm[...]))
+        add_fold(wt, gqm)
         mirror_wait(2)
         north = mirrored(2)
         for b in range(3):
             sx[b * C:(b + 1) * C, slot(H)] = north[:, b * W:(b + 1) * W]
 
-    side_sum_lon()
     for r, value in enumerate(shift_sum()):
         fh[:, slot(r)] = (value * ocean(r) * slope[:, r * W:(r + 1) * W]).astype(BF16)
 
     mirror_send(1, fh)
+
+    @pl.when(m == NM - 1)
+    def _():
+        side_send(0)
+
     tap_grad(fh, sx)
     tap_store()
     sum_start()
@@ -650,7 +666,7 @@
     @pl.when(top)
     def _():
         mirror_wait(1)
-        add_fold(dot(wp[...], fold_rows(mirrored(1))))
+        add_fold(wp, fold_rows(mirrored(1)))
 
     cells[...] = g_ref[...].astype(F32).reshape(C * H, W)
     for r, value in enumerate(shift_sum()):

time: 47.8 us -> 46.6 us (0.975)
  Pallas kernels: 46.5 us -> 45.6 us
    pallas_call x1, Pallas kernels: 44.6 us -> 43.7 us  [body(): pl.pallas_call(functools.partial(kernel, cfg), out_shape=shapes, in_specs...]
where the time goes in v5:
time: 46.6 us; the launch traced here: 46.4 us
  Pallas kernels  45.6 us (98%)
  between operations  0.8 us (2%)
    pallas_call x1, Pallas kernels, body(): pl.pallas_call(functools.partial(kernel, cfg), out_shape=shapes, in_specs...  43.7 us
    pallas_call x1, Pallas kernels, body(): pl.pallas_call(hand_over, out_shape=shapes, in_specs=[pl.BlockSpec(memory...  1.89 us

profile of v5, /device:TPU:6, one launch (start us, length us, event | category | flops | bytes accessed | tf_op | source)
XLA Modules:
  0.0 46.4 jit_solution(13442409866011807625)
XLA Ops:
  0.6 43.7 %shard_map.112 = (f32[1280,128]{1,0:T(8,128)}, f32[3,10,3,10]{3,2,1,0:T(4,128)}, f32[3,10,3,10]{3,2,1,0:T(4,128)}) custom-call(bf16[160,8,128]{2,1,0:T(8,128)(2,1)} %x_hbm.1, f32[8,160]{1,0:T(8,128)} %bitcast.10, bf16[160,8,128]{2,1,0:T(8,128)(2,1)} %h_hbm.1, f32[8,160]{1,0:T(8,128)} %bitcast.11, bf16[160,8,128]{2,1,0:T(8,128)(2,1)} %g_hbm.1, ...), custom_call_target="tpu_custom_call" | custom-call | tf_op jit(solution)/shard_map/pallas_call | solution.py:795
  44.4 1.9 %shard_map.113 = (f32[1280,128]{1,0:T(8,128)}, f32[3,10,3,10]{3,2,1,0:T(4,128)}, f32[3,10,3,10]{3,2,1,0:T(4,128)}) custom-call(f32[1280,128]{1,0:T(8,128)} %get-tuple-element.9.out_in, f32[3,10,3,10]{3,2,1,0:T(4,128)} %get-tuple-element.10.first_in, f32[3,10,3,10]{3,2,1,0:T(4,128)} %get-tuple-element.11.second_in), custom_call_target="tpu_custom_call" | custom-call | tf_op jit(solution)/shard_map/pallas_call | solution.py:805

commit v6 on v5

--- a/solution.py
+++ b/solution.py
@@ -496,16 +496,16 @@
             for a in range(3):
                 for b in range(3):
                     put_wide(tiles, slane, sources[a], b * C + s * CI, CI, (3 * a + b) * CI)
-            small[s] = tiles[0]
+            small[s] = tiles[0].astype(SUM_TYPE)
         small_in[i] = small[i]
         for d in lon_order:
             lon_copy(d, None).start()
 
     def sum_end():
         each(1, NI, lambda d: lon_copy(d, lon(d)).wait_recv())
-        total = small_in[0]
+        total = small_in[0].astype(F32)
         for s in range(1, NI):
-            total = total + small_in[s]
+            total = total + small_in[s].astype(F32)
         total = total * cfg["factor"]
         for a in range(3):
             for b in range(3):
@@ -777,8 +777,8 @@
         vm((NM, RB, LA), SUM_TYPE),
         vm((NM, RB, LA), SUM_TYPE),
         vm((RB + PAD, LA), F32),
-        vm((NI, PAD, LANES), F32),
-        vm((NI, PAD, LANES), F32),
+        vm((NI, PAD, LANES), SUM_TYPE),
+        vm((NI, PAD, LANES), SUM_TYPE),
         vm((LANES, LANES), F32),
         vm((NI, RB, LA), F32),
         vm((NI, RB // 2, LA), SUM_TYPE),

time: 46.6 us -> 45.9 us (0.985)
  Pallas kernels: 45.6 us -> 44.7 us
    pallas_call x1, Pallas kernels: 43.7 us -> 42.8 us  [body(): pl.pallas_call(functools.partial(kernel, cfg), out_shape=shapes, in_specs...]
where the time goes in v6:
time: 45.9 us; the launch traced here: 45.4 us
  Pallas kernels  44.7 us (97%)
  between operations  0.64 us (1%)
    pallas_call x1, Pallas kernels, body(): pl.pallas_call(functools.partial(kernel, cfg), out_shape=shapes, in_specs...  42.8 us
    pallas_call x1, Pallas kernels, body(): pl.pallas_call(hand_over, out_shape=shapes, in_specs=[pl.BlockSpec(memory...  1.89 us

profile of v6, /device:TPU:6, one launch (start us, length us, event | category | flops | bytes accessed | tf_op | source)
XLA Modules:
  0.0 45.4 jit_solution(9326921154589651004)
XLA Ops:
  0.6 42.8 %shard_map.112 = (f32[1280,128]{1,0:T(8,128)}, f32[3,10,3,10]{3,2,1,0:T(4,128)}, f32[3,10,3,10]{3,2,1,0:T(4,128)}) custom-call(bf16[160,8,128]{2,1,0:T(8,128)(2,1)} %x_hbm.1, f32[8,160]{1,0:T(8,128)} %bitcast.10, bf16[160,8,128]{2,1,0:T(8,128)(2,1)} %h_hbm.1, f32[8,160]{1,0:T(8,128)} %bitcast.11, bf16[160,8,128]{2,1,0:T(8,128)(2,1)} %g_hbm.1, ...), custom_call_target="tpu_custom_call" | custom-call | tf_op jit(solution)/shard_map/pallas_call | solution.py:795
  43.5 1.9 %shard_map.113 = (f32[1280,128]{1,0:T(8,128)}, f32[3,10,3,10]{3,2,1,0:T(4,128)}, f32[3,10,3,10]{3,2,1,0:T(4,128)}) custom-call(f32[1280,128]{1,0:T(8,128)} %get-tuple-element.9.out_in, f32[3,10,3,10]{3,2,1,0:T(4,128)} %get-tuple-element.10.first_in, f32[3,10,3,10]{3,2,1,0:T(4,128)} %get-tuple-element.11.second_in), custom_call_target="tpu_custom_call" | custom-call | tf_op jit(solution)/shard_map/pallas_call | solution.py:805

commit v7 on v6

--- a/solution.py
+++ b/solution.py
@@ -105,7 +105,7 @@
 
     lon_order = [d for d in (9, 8, 11, 10, 7, 6, 15, 14, 5, 13, 4, 12, 3, 2, 1) if d < NI]
     lat_order = [d for d in (12, 13, 10, 11, 14, 15, 8, 9, 4, 5, 2, 3, 6, 7, 1) if d < NJ]
-    mate_order = [d for d in (6, 5, 7, 4, 2, 1, 3) if d < NM]
+    mate_order = [d for d in (4, 6, 5, 7, 2, 1, 3) if d < NM]
 
     barrier = pltpu.get_barrier_semaphore()
 
@@ -498,7 +498,7 @@
                     put_wide(tiles, slane, sources[a], b * C + s * CI, CI, (3 * a + b) * CI)
             small[s] = tiles[0].astype(SUM_TYPE)
         small_in[i] = small[i]
-        for d in lon_order:
+        for d in sorted(lon_order, key=lambda d: d % 2 == 0):
             lon_copy(d, None).start()
 
     def sum_end():
@@ -645,8 +645,8 @@
         packed = add_edges(packed, 0, r, fh[:, slot(r)].astype(F32))
     turn_edges(1, packed)
     late = halo_copies(1, (fh,))
+    sum_chips()
     halo_start(late)
-    sum_chips()
 
 
     pass_on(0)

time: 45.9 us -> 45.6 us (level)
  no operation moved by 1% of the time
where the time goes in v7:
time: 45.6 us; the launch traced here: 45.4 us
  Pallas kernels  44.8 us (98%)
  between operations  0.64 us (1%)
    pallas_call x1, Pallas kernels, body(): pl.pallas_call(functools.partial(kernel, cfg), out_shape=shapes, in_specs...  42.9 us
    pallas_call x1, Pallas kernels, body(): pl.pallas_call(hand_over, out_shape=shapes, in_specs=[pl.BlockSpec(memory...  1.89 us

profile of v7, /device:TPU:6, one launch (start us, length us, event | category | flops | bytes accessed | tf_op | source)
XLA Modules:
  0.0 45.4 jit_solution(3033807805214077002)
XLA Ops:
  0.6 42.9 %shard_map.112 = (f32[1280,128]{1,0:T(8,128)}, f32[3,10,3,10]{3,2,1,0:T(4,128)}, f32[3,10,3,10]{3,2,1,0:T(4,128)}) custom-call(bf16[160,8,128]{2,1,0:T(8,128)(2,1)} %x_hbm.1, f32[8,160]{1,0:T(8,128)} %bitcast.10, bf16[160,8,128]{2,1,0:T(8,128)(2,1)} %h_hbm.1, f32[8,160]{1,0:T(8,128)} %bitcast.11, bf16[160,8,128]{2,1,0:T(8,128)(2,1)} %g_hbm.1, ...), custom_call_target="tpu_custom_call" | custom-call | tf_op jit(solution)/shard_map/pallas_call | solution.py:795
  43.5 1.9 %shard_map.113 = (f32[1280,128]{1,0:T(8,128)}, f32[3,10,3,10]{3,2,1,0:T(4,128)}, f32[3,10,3,10]{3,2,1,0:T(4,128)}) custom-call(f32[1280,128]{1,0:T(8,128)} %get-tuple-element.9.out_in, f32[3,10,3,10]{3,2,1,0:T(4,128)} %get-tuple-element.10.first_in, f32[3,10,3,10]{3,2,1,0:T(4,128)} %get-tuple-element.11.second_in), custom_call_target="tpu_custom_call" | custom-call | tf_op jit(solution)/shard_map/pallas_call | solution.py:805

commit v8 on v7

--- a/solution.py
+++ b/solution.py
@@ -176,15 +176,12 @@
     for load in loads[2:6]:
         load.wait()
     scale = jnp.transpose(xs_ref[...])
-    packed = jnp.zeros((C, W), F32)
     for r, blk in enumerate(blocks(g_ref)):
         value = blk * ocean(r)
         fy[:, slot(r)] = value.astype(BF16)
-        packed = add_edges(packed, 0, r, value)
     for r, blk in enumerate(blocks(x_ref)):
         x = (blk * scale[:, r:r + 1]).astype(BF16)
         sx[center, slot(r)] = x
-        packed = add_edges(packed, 1, r, x.astype(F32))
 
     pl.semaphore_wait(barrier, NI - 1 + NJ - 1 + 4)
 
@@ -265,19 +262,7 @@
         return jnp.concatenate([before, block, after], axis=1).astype(BF16)
 
     mirror_send(0, fy)
-    loads[1].wait()
-    wown[0] = make_tile(w0_ref).astype(BF16)
-
-    for load in loads[6:]:
-        load.wait()
-    scale = jnp.transpose(hs_ref[...])
-    for r, blk in enumerate(blocks(h_ref)):
-        h = blk * scale[:, r:r + 1]
-        value, deriv = gelu_parts(h)
-        act[:, r * W:(r + 1) * W] = (ocean(r) * value).astype(BF16)
-        slope[:, r * W:(r + 1) * W] = deriv
-    turn_edges(0, packed)
-
+    mirror_send(2, sx.at[center])
     def halo_copies(phase, fields):
         north, south = jnp.logical_not(top), jnp.logical_not(bottom)
         out = []
@@ -318,9 +303,26 @@
             only(sent, copy.wait_send)
 
     early = halo_copies(0, (fy, sx.at[center]))
-    halo_start(early)
-
-    mirror_send(2, sx.at[center])
+    halo_start(early[:4])
+    packed = jnp.zeros((C, W), F32)
+    for r in range(H):
+        packed = add_edges(packed, 0, r, fy[:, slot(r)].astype(F32))
+        packed = add_edges(packed, 1, r, sx[center, slot(r)].astype(F32))
+    turn_edges(0, packed)
+    halo_start(early[4:])
+    loads[1].wait()
+    wown[0] = make_tile(w0_ref).astype(BF16)
+
+    for load in loads[6:]:
+        load.wait()
+    scale = jnp.transpose(hs_ref[...])
+    for r, blk in enumerate(blocks(h_ref)):
+        h = blk * scale[:, r:r + 1]
+        value, deriv = gelu_parts(h)
+        act[:, r * W:(r + 1) * W] = (ocean(r) * value).astype(BF16)
+        slope[:, r * W:(r + 1) * W] = deriv
+
+
     for d in lon_order:
         tile_copy(0, d, None).start()
     wtile[0, i] = wown[0]

time: 45.6 us -> 45.3 us (level)
  no operation moved by 1% of the time
where the time goes in v8:
time: 45.3 us; the launch traced here: 45.2 us
  Pallas kernels  44.6 us (98%)
  between operations  0.64 us (1%)
    pallas_call x1, Pallas kernels, body(): pl.pallas_call(functools.partial(kernel, cfg), out_shape=shapes, in_specs...  42.7 us
    pallas_call x1, Pallas kernels, body(): pl.pallas_call(hand_over, out_shape=shapes, in_specs=[pl.BlockSpec(memory...  1.89 us

profile of v8, /device:TPU:6, one launch (start us, length us, event | category | flops | bytes accessed | tf_op | source)
XLA Modules:
  0.0 45.2 jit_solution(5350612626396357434)
XLA Ops:
  0.6 42.7 %shard_map.112 = (f32[1280,128]{1,0:T(8,128)}, f32[3,10,3,10]{3,2,1,0:T(4,128)}, f32[3,10,3,10]{3,2,1,0:T(4,128)}) custom-call(bf16[160,8,128]{2,1,0:T(8,128)(2,1)} %x_hbm.1, f32[8,160]{1,0:T(8,128)} %bitcast.10, bf16[160,8,128]{2,1,0:T(8,128)(2,1)} %h_hbm.1, f32[8,160]{1,0:T(8,128)} %bitcast.11, bf16[160,8,128]{2,1,0:T(8,128)(2,1)} %g_hbm.1, ...), custom_call_target="tpu_custom_call" | custom-call | tf_op jit(solution)/shard_map/pallas_call | solution.py:797
  43.3 1.9 %shard_map.113 = (f32[1280,128]{1,0:T(8,128)}, f32[3,10,3,10]{3,2,1,0:T(4,128)}, f32[3,10,3,10]{3,2,1,0:T(4,128)}) custom-call(f32[1280,128]{1,0:T(8,128)} %get-tuple-element.9.out_in, f32[3,10,3,10]{3,2,1,0:T(4,128)} %get-tuple-element.10.first_in, f32[3,10,3,10]{3,2,1,0:T(4,128)} %get-tuple-element.11.second_in), custom_call_target="tpu_custom_call" | custom-call | tf_op jit(solution)/shard_map/pallas_call | solution.py:807
